TPU v7x, 256 devices: a whole 4x4x8 slice. The times are simulated.
256 devices in a mesh: gx: 16 (over x, z_hi), gy: 16 (over y, z_lo, core).
Axes of the slice: x: 4, y: 4, z: 8 (z_hi: 4, z_lo: 2; z = z_hi * 2 + z_lo), core: 2. Of those that a mesh axis runs over, the one named last changes fastest.
Arguments:
- right_side: float32 [3, 128, 512, 128], P(None, 'gx', 'gy'), may hold values from -6 to 6
- classes: int32 [128, 512, 128], P('gx', 'gy'), may hold values from 0 to 15
- table: float32 [16], replicated, may hold values from 0.05 to 4
Outputs:
- correction: float32 [3, 128, 512, 128], P(None, 'gx', 'gy')
All inputs are finite; a program needn't handle non-finite values.
Results may differ from a plain program's by a relative error of at most 0.000026.
Values sent between devices are 32-bit elements; how exact they have to be, the bound alone decides.
A program may use at most 64 MiB of HBM per device.

v0:
```python
import jax
import jax.numpy as jnp
from jax import lax
from jax.sharding import PartitionSpec as P

EDGE_SWEEPS = 4
NODE_SWEEPS = 4
COARSE_SWEEPS = 8


edge_top = 20.0
node_top = 48.0
coarse_top = 96.0


def with_halo(block, sides, width):
    for axis, dim in sides:
        count = lax.axis_size(axis)
        forward = [(i, i + 1) for i in range(count - 1)]
        backward = [(target, source) for source, target in forward]
        low = lax.ppermute(
            lax.slice_in_dim(block, block.shape[dim] - width, None, axis=dim), axis, forward
        )
        high = lax.ppermute(lax.slice_in_dim(block, 0, width, axis=dim), axis, backward)
        block = jnp.concatenate([low, block, high], axis=dim)
    return block


def shifted(value, axis, steps):
    count = lax.axis_size(axis)
    initial, last = (max(0, -steps), min(count, count - steps))
    return lax.ppermute(value, axis, [(source, source + steps) for source in range(initial, last)])


def ahead(field, axis):
    count = field.shape[axis]
    tail = jnp.zeros_like(lax.slice_in_dim(field, 0, 1, axis=axis))
    return jnp.concatenate([lax.slice_in_dim(field, 1, count, axis=axis), tail], axis=axis)


def behind(field, axis):
    count = field.shape[axis]
    head = jnp.zeros_like(lax.slice_in_dim(field, 0, 1, axis=axis))
    return jnp.concatenate([head, lax.slice_in_dim(field, 0, count - 1, axis=axis)], axis=axis)


def forward(field, axis):
    return ahead(field, axis) - field


def adjoint(field, axis):
    return behind(field, axis) - field


def curl(edges):
    return jnp.stack(
        [
            forward(edges[2], 1) - forward(edges[1], 2),
            forward(edges[0], 2) - forward(edges[2], 0),
            forward(edges[1], 0) - forward(edges[0], 1),
        ]
    )


def curl_adjoint(faces):
    return jnp.stack(
        [
            adjoint(faces[2], 1) - adjoint(faces[1], 2),
            adjoint(faces[0], 2) - adjoint(faces[2], 0),
            adjoint(faces[1], 0) - adjoint(faces[0], 1),
        ]
    )


def gradient(nodes):
    return jnp.stack([forward(nodes, 0), forward(nodes, 1), forward(nodes, 2)])


def divergence(edges):
    return adjoint(edges[0], 0) + adjoint(edges[1], 1) + adjoint(edges[2], 2)


def chebyshev(apply, rhs, top, ratio, count, need_residual):
    low = top / ratio
    center = 0.5 * (top + low)
    radius = 0.5 * (top - low)
    sharp = center / radius
    rho = 1.0 / sharp
    update = rhs / center
    result = update
    residual = rhs - apply(update)
    for turn in range(1, count):
        rho_next = 1.0 / (2.0 * sharp - rho)
        update = rho_next * rho * update + 2.0 * rho_next / radius * residual
        result = result + update
        if turn + 1 < count or need_residual:
            residual = residual - apply(update)
        rho = rho_next
    return (result, residual)


def lower_pad(field, axis):
    head = jnp.zeros_like(lax.slice_in_dim(field, 0, 1, axis=axis))
    return jnp.concatenate([head, field], axis=axis)


def upper_pad(field, axis):
    tail = jnp.zeros_like(lax.slice_in_dim(field, 0, 1, axis=axis))
    return jnp.concatenate([field, tail], axis=axis)


def reduce_pairs(field, axis):
    count = field.shape[axis]
    lower = lax.slice_in_dim(field, 0, 1, axis=axis)
    even = lax.slice_in_dim(field, 1, count, 2, axis=axis)
    odd = lax.slice_in_dim(field, 2, count, 2, axis=axis)
    before = jnp.concatenate(
        [lower, lax.slice_in_dim(odd, 0, odd.shape[axis] - 1, axis=axis)], axis=axis
    )
    return even + 0.5 * (odd + before)


def spread_pairs(field, axis):
    count = field.shape[axis]
    own = lax.slice_in_dim(field, 0, count - 1, axis=axis)
    upper = lax.slice_in_dim(field, 1, count, axis=axis)
    middle = 0.5 * (own + upper)
    joined = jnp.stack([own, middle], axis=axis + 1)
    shape = list(own.shape)
    shape[axis] = shape[axis] * 2
    return joined.reshape(shape)


def block_mean(field):
    a_len, b_len, c_len = field.shape
    return field.reshape(a_len // 2, 2, b_len // 2, 2, c_len // 2, 2).mean(axis=(1, 3, 5))


def inside_mask(cx_len, cy_len, width):
    rows = lax.axis_index("gx") * cx_len - width + jnp.arange(cx_len + 2 * width, dtype=jnp.int32)
    cols = lax.axis_index("gy") * cy_len - width + jnp.arange(cy_len + 2 * width, dtype=jnp.int32)
    inside_rows = (rows >= 0) & (rows < cx_len * lax.axis_size("gx"))
    inside_cols = (cols >= 0) & (cols < cy_len * lax.axis_size("gy"))
    return (inside_rows[:, None] & inside_cols[None, :]).astype(jnp.float32)[None, :, :, None]


def shards(right_side, classes, table):
    kinds = jnp.arange(table.shape[0], dtype=jnp.int32)
    sigma = jnp.sum(
        jnp.where(classes[None] == kinds[:, None, None, None], table[:, None, None, None], 0.0),
        axis=0,
    )
    cx_len, cy_len, nz_len = sigma.shape
    rim_mask = inside_mask(cx_len, cy_len, 1)

    def apply_edges(edges):
        padded = with_halo(edges, (("gx", 1), ("gy", 2)), 1)
        return curl_adjoint(curl(padded) * rim_mask)[:, 1:-1, 1:-1] + sigma[None] * edges

    edge_smooth, edge_residual = chebyshev(
        apply_edges, right_side, edge_top, 30.0, EDGE_SWEEPS, True
    )
    stacked = jnp.concatenate([edge_residual, sigma[None]], axis=0)
    below_x = shifted(stacked[:, -2:], "gx", 1)
    extended = jnp.concatenate([below_x, stacked], axis=1)
    below_y = shifted(extended[:, :, -2:], "gy", 1)
    extended = jnp.concatenate([below_y, extended], axis=2)
    residual_low = extended[0:3]
    sigma_low = extended[3]
    nodal_rhs = -divergence(residual_low[:, 1:, 1:])[1:, 1:]
    node_sigma = jnp.pad(sigma_low[1:, 1:], ((0, 1), (0, 1), (0, 0)))[None]

    def apply_nodes(nodes):
        padded = with_halo(nodes, (("gx", 0), ("gy", 1)), 1)
        return -divergence(node_sigma * gradient(padded))[1:-1, 1:-1]

    node_smooth, node_residual = chebyshev(
        apply_nodes, nodal_rhs, node_top, 30.0, NODE_SWEEPS, True
    )
    reduced = reduce_pairs(lower_pad(node_residual, 2), 2)
    lower_x = shifted(reduced[-1:], "gx", 1)
    reduced = jnp.concatenate([lower_x, reduced], axis=0)
    lower_y = shifted(reduced[:, -1:], "gy", 1)
    reduced = jnp.concatenate([lower_y, reduced], axis=1)
    reduced = reduce_pairs(reduced, 0)
    coarse_rhs = reduce_pairs(reduced, 1)
    coarse_low = block_mean(sigma_low)
    grid_sigma = jnp.pad(coarse_low, ((0, 1), (0, 1), (0, 0)))[None]

    def apply_coarse(nodes):
        padded = with_halo(nodes, (("gx", 0), ("gy", 1)), 1)
        return -2.0 * divergence(grid_sigma * gradient(padded))[1:-1, 1:-1]

    coarse_answer, spare = chebyshev(
        apply_coarse, coarse_rhs, coarse_top, 100.0, COARSE_SWEEPS, False
    )
    upper_x = shifted(coarse_answer[0:1], "gx", -1)
    widened = jnp.concatenate([coarse_answer, upper_x], axis=0)
    upper_y = shifted(widened[:, 0:1], "gy", -1)
    widened = jnp.concatenate([widened, upper_y], axis=1)
    fine = spread_pairs(widened, 0)
    fine = spread_pairs(fine, 1)
    fine = spread_pairs(upper_pad(fine, 2), 2)
    potential = node_smooth + fine
    next_x = shifted(potential[0:1], "gx", -1)
    next_y = shifted(potential[:, 0:1], "gy", -1)
    grad_field = jnp.stack(
        [
            jnp.concatenate([potential[1:], next_x], axis=0) - potential,
            jnp.concatenate([potential[:, 1:], next_y], axis=1) - potential,
            forward(potential, 2),
        ]
    )
    return edge_smooth + grad_field


def solution(mesh):
    return jax.shard_map(
        shards,
        mesh=mesh,
        in_specs=(P(None, "gx", "gy", None), P("gx", "gy", None), P()),
        out_specs=P(None, "gx", "gy", None),
        check_vma=False,
    )
```

profile of v0, /device:TPU:35, one launch (start us, length us, event | category | flops | bytes accessed | tf_op | source)
XLA Modules:
  0.0 388.4 jit_solution(18058457531118828703)
XLA Ops:
  1.3 4.9 %collective-permute-start = (f32[3,1,32,128]{3,1,2,0:T(1,128)S(1)}, f32[3,1,32,128]{3,1,2,0:T(1,128)S(1)}, u32[]{:S(2)}, u32[]{:S(2)}) collective-permute-start(f32[3,1,32,128]{3,1,2,0:T(1,128)S(1)} %get-tuple-element.124), channel_id=1, source_target_pairs={{0,16},{16,32},{32,48},{48,64},{64,80},{80,96},{96,112},{112,128},... | collective-permute-start | bytes 147464 | tf_op jit(solution)/shard_map/ppermute | solution.py:21
  6.2 4.0 %collective-permute-start.1 = (f32[3,1,32,128]{3,1,2,0:T(1,128)S(1)}, f32[3,1,32,128]{3,1,2,0:T(1,128)S(1)}, u32[]{:S(2)}, u32[]{:S(2)}) collective-permute-start(f32[3,1,32,128]{3,1,2,0:T(1,128)S(1)} %get-tuple-element.125), channel_id=1, source_target_pairs={{16,0},{32,16},{48,32},{64,48},{80,64},{96,80},{112,96},{128,112},... | collective-permute-start | bytes 147464 | tf_op jit(solution)/shard_map/ppermute | solution.py:24
  13.0 5.4 %collective-permute-start.2 = (f32[3,10,1,128]{3,1,2,0:T(8,128)S(1)}, f32[3,10,1,128]{3,1,2,0:T(8,128)S(1)}, u32[]{:S(2)}, u32[]{:S(2)}) collective-permute-start(f32[3,10,1,128]{3,1,2,0:T(8,128)S(1)} %get-tuple-element.116), channel_id=1, source_target_pairs={{0,1},{1,2},{2,3},{3,4},{4,5},{5,6},{6,7},{7,8},{8,9},{9,10},{10,1... | collective-permute-start | bytes 46088 | tf_op jit(solution)/shard_map/ppermute | solution.py:21
  20.5 3.9 %collective-permute-done.3 = f32[3,10,1,128]{3,1,2,0:T(8,128)S(1)} collective-permute-done((f32[3,10,1,128]{3,1,2,0:T(8,128)S(1)}, f32[3,10,1,128]{3,1,2,0:T(8,128)S(1)}, u32[]{:S(2)}, u32[]{:S(2)}) %collective-permute-start.3) | collective-permute-done | bytes 15392 | tf_op jit(solution)/shard_map/ppermute | solution.py:24
  26.8 6.2 %collective-permute-start.4 = (f32[3,1,32,128]{3,1,2,0:T(1,128)S(1)}, f32[3,1,32,128]{3,1,2,0:T(1,128)S(1)}, u32[]{:S(2)}, u32[]{:S(2)}) collective-permute-start(f32[3,1,32,128]{3,1,2,0:T(1,128)S(1)} %get-tuple-element.122), channel_id=1, source_target_pairs={{0,16},{16,32},{32,48},{48,64},{64,80},{80,96},{96,112},{112,128},... | collective-permute-start | bytes 147464 | tf_op jit(solution)/shard_map/ppermute | solution.py:21
  35.2 3.6 collective-permute-done.5
  44.2 4.0 %collective-permute-done.7 = f32[3,10,1,128]{3,1,2,0:T(8,128)S(1)} collective-permute-done((f32[3,10,1,128]{3,1,2,0:T(8,128)S(1)}, f32[3,10,1,128]{3,1,2,0:T(8,128)S(1)}, u32[]{:S(2)}, u32[]{:S(2)}) %collective-permute-start.7) | collective-permute-done | bytes 15392 | tf_op jit(solution)/shard_map/ppermute | solution.py:24
  53.3 5.2 %collective-permute-start.9 = (f32[3,1,32,128]{3,1,2,0:T(1,128)S(1)}, f32[3,1,32,128]{3,1,2,0:T(1,128)S(1)}, u32[]{:S(2)}, u32[]{:S(2)}) collective-permute-start(f32[3,1,32,128]{3,1,2,0:T(1,128)S(1)} %get-tuple-element.121), channel_id=1, source_target_pairs={{16,0},{32,16},{48,32},{64,48},{80,64},{96,80},{112,96},{128,112},... | collective-permute-start | bytes 147464 | tf_op jit(solution)/shard_map/ppermute | solution.py:24
  64.6 4.1 %collective-permute-done.11 = f32[3,10,1,128]{3,1,2,0:T(8,128)S(1)} collective-permute-done((f32[3,10,1,128]{3,1,2,0:T(8,128)S(1)}, f32[3,10,1,128]{3,1,2,0:T(8,128)S(1)}, u32[]{:S(2)}, u32[]{:S(2)}) %collective-permute-start.11) | collective-permute-done | bytes 15392 | tf_op jit(solution)/shard_map/ppermute | solution.py:24
  70.4 3.5 collective-permute-start.12
  74.0 5.4 %collective-permute-start.13 = (f32[3,1,32,128]{3,1,2,0:T(1,128)S(1)}, f32[3,1,32,128]{3,1,2,0:T(1,128)S(1)}, u32[]{:S(2)}, u32[]{:S(2)}) collective-permute-start(f32[3,1,32,128]{3,1,2,0:T(1,128)S(1)} %get-tuple-element.119), channel_id=1, source_target_pairs={{16,0},{32,16},{48,32},{64,48},{80,64},{96,80},{112,96},{128,112},... | collective-permute-start | bytes 147464 | tf_op jit(solution)/shard_map/ppermute | solution.py:24
  85.3 4.0 %collective-permute-done.15 = f32[3,10,1,128]{3,1,2,0:T(8,128)S(1)} collective-permute-done((f32[3,10,1,128]{3,1,2,0:T(8,128)S(1)}, f32[3,10,1,128]{3,1,2,0:T(8,128)S(1)}, u32[]{:S(2)}, u32[]{:S(2)}) %collective-permute-start.15) | collective-permute-done | bytes 15392 | tf_op jit(solution)/shard_map/ppermute | solution.py:24
  91.0 5.1 %collective-permute-start.16 = (f32[4,2,32,128]{3,1,2,0:T(2,128)S(1)}, f32[4,2,32,128]{3,1,2,0:T(2,128)S(1)}, u32[]{:S(2)}, u32[]{:S(2)}) collective-permute-start(f32[4,2,32,128]{3,1,2,0:T(2,128)S(1)} %pad_maximum_fusion.20), channel_id=1, source_target_pairs={{0,16},{16,32},{32,48},{48,64},{64,80},{80,96},{96,112},{112,128},... | collective-permute-start | bytes 393224 | tf_op jit(solution)/shard_map/ppermute | solution.py:32
  96.1 4.3 %collective-permute-done.16 = f32[4,2,32,128]{3,1,2,0:T(2,128)S(1)} collective-permute-done((f32[4,2,32,128]{3,1,2,0:T(2,128)S(1)}, f32[4,2,32,128]{3,1,2,0:T(2,128)S(1)}, u32[]{:S(2)}, u32[]{:S(2)}) %collective-permute-start.16) | collective-permute-done | bytes 131104 | tf_op jit(solution)/shard_map/ppermute | solution.py:32
  107.9 5.8 %collective-permute-start.19 = (f32[1,32,128]{2,0,1:T(1,128)S(1)}, f32[1,32,128]{2,0,1:T(1,128)S(1)}, u32[]{:S(2)}, u32[]{:S(2)}) collective-permute-start(f32[1,32,128]{2,0,1:T(1,128)S(1)} %get-tuple-element.181), channel_id=1, source_target_pairs={{16,0},{32,16},{48,32},{64,48},{80,64},{96,80},{112,96},{128,112},... | collective-permute-start | bytes 49160 | tf_op jit(solution)/shard_map/ppermute | solution.py:24
  116.6 6.1 %collective-permute-start.20 = (f32[10,1,128]{2,0,1:T(8,128)S(1)}, f32[10,1,128]{2,0,1:T(8,128)S(1)}, u32[]{:S(2)}, u32[]{:S(2)}) collective-permute-start(f32[10,1,128]{2,0,1:T(8,128)S(1)} %get-tuple-element.169), channel_id=1, source_target_pairs={{0,1},{1,2},{2,3},{3,4},{4,5},{5,6},{6,7},{7,8},{8,9},{9,10},{10,1... | collective-permute-start | bytes 15368 | tf_op jit(solution)/shard_map/ppermute | solution.py:21
  124.8 3.8 collective-permute-done.21
  129.3 5.6 %collective-permute-start.22 = (f32[1,32,128]{2,0,1:T(1,128)S(1)}, f32[1,32,128]{2,0,1:T(1,128)S(1)}, u32[]{:S(2)}, u32[]{:S(2)}) collective-permute-start(f32[1,32,128]{2,0,1:T(1,128)S(1)} %get-tuple-element.178), channel_id=1, source_target_pairs={{0,16},{16,32},{32,48},{48,64},{64,80},{80,96},{96,112},{112,128},... | collective-permute-start | bytes 49160 | tf_op jit(solution)/shard_map/ppermute | solution.py:21
  145.7 3.9 %collective-permute-done.25 = f32[10,1,128]{2,0,1:T(8,128)S(1)} collective-permute-done((f32[10,1,128]{2,0,1:T(8,128)S(1)}, f32[10,1,128]{2,0,1:T(8,128)S(1)}, u32[]{:S(2)}, u32[]{:S(2)}) %collective-permute-start.25) | collective-permute-done | bytes 5152 | tf_op jit(solution)/shard_map/ppermute | solution.py:24
  153.2 5.4 %collective-permute-start.27 = (f32[1,32,128]{2,0,1:T(1,128)S(1)}, f32[1,32,128]{2,0,1:T(1,128)S(1)}, u32[]{:S(2)}, u32[]{:S(2)}) collective-permute-start(f32[1,32,128]{2,0,1:T(1,128)S(1)} %get-tuple-element.177), channel_id=1, source_target_pairs={{16,0},{32,16},{48,32},{64,48},{80,64},{96,80},{112,96},{128,112},... | collective-permute-start | bytes 49160 | tf_op jit(solution)/shard_map/ppermute | solution.py:24
  164.5 3.9 %collective-permute-done.29 = f32[10,1,128]{2,0,1:T(8,128)S(1)} collective-permute-done((f32[10,1,128]{2,0,1:T(8,128)S(1)}, f32[10,1,128]{2,0,1:T(8,128)S(1)}, u32[]{:S(2)}, u32[]{:S(2)}) %collective-permute-start.29) | collective-permute-done | bytes 5152 | tf_op jit(solution)/shard_map/ppermute | solution.py:24
  172.5 5.5 %collective-permute-start.31 = (f32[1,32,128]{2,0,1:T(1,128)S(1)}, f32[1,32,128]{2,0,1:T(1,128)S(1)}, u32[]{:S(2)}, u32[]{:S(2)}) collective-permute-start(f32[1,32,128]{2,0,1:T(1,128)S(1)} %get-tuple-element.175), channel_id=1, source_target_pairs={{16,0},{32,16},{48,32},{64,48},{80,64},{96,80},{112,96},{128,112},... | collective-permute-start | bytes 49160 | tf_op jit(solution)/shard_map/ppermute | solution.py:24
  183.8 3.7 collective-permute-done.33
  193.1 4.9 %collective-permute-start.34 = (f32[1,32,64]{2,0,1:T(1,128)S(1)}, f32[1,32,64]{2,0,1:T(1,128)S(1)}, u32[]{:S(2)}, u32[]{:S(2)}) collective-permute-start(f32[1,32,64]{2,0,1:T(1,128)S(1)} %slice.1415), channel_id=1, source_target_pairs={{0,16},{16,32},{32,48},{48,64},{64,80},{80,96},{96,112},{112,128},... | collective-permute-start | bytes 24584 | tf_op jit(solution)/shard_map/ppermute | solution.py:32
  208.3 5.8 %collective-permute-start.37 = (f32[1,16,64]{2,0,1:T(1,128)S(1)}, f32[1,16,64]{2,0,1:T(1,128)S(1)}, u32[]{:S(2)}, u32[]{:S(2)}) collective-permute-start(f32[1,16,64]{2,0,1:T(1,128)S(1)} %get-tuple-element.241), channel_id=1, source_target_pairs={{16,0},{32,16},{48,32},{64,48},{80,64},{96,80},{112,96},{128,112},... | collective-permute-start | bytes 12296 | tf_op jit(solution)/shard_map/ppermute | solution.py:24
  214.2 12.7 %reshape_squeeze.3 = f32[5,2,17,2,64,2]{5,4,3,2,1,0:T(8,128)} reshape(f32[1,10,34,128]{3,2,1,0:T(8,128)S(1)} %copy.44) | data formatting | bytes 348160 | tf_op jit(solution)/shard_map/reshape;squeeze | solution.py:136
  226.9 5.0 %reduce_sum.19 = f32[5,17,64]{2,1,0:T(8,128)S(1)} reduce(f32[5,2,17,2,64,2]{5,4,3,2,1,0:T(8,128)} %reshape_squeeze.3, f32[]{:T(128)} %constant.41.clone.1), dimensions={1,3,5}, to_apply=%region_1.2 | reduce | flops 38080 | bytes 195844 | tf_op jit(solution)/shard_map/reduce_sum | solution.py:136
  232.0 5.7 %collective-permute-start.38 = (f32[6,1,64]{2,0,1:T(8,128)S(1)}, f32[6,1,64]{2,0,1:T(8,128)S(1)}, u32[]{:S(2)}, u32[]{:S(2)}) collective-permute-start(f32[6,1,64]{2,0,1:T(8,128)S(1)} %get-tuple-element.226), channel_id=1, source_target_pairs={{0,1},{1,2},{2,3},{3,4},{4,5},{5,6},{6,7},{7,8},{8,9},{9,10},{10,1... | collective-permute-start | bytes 4616 | tf_op jit(solution)/shard_map/ppermute | solution.py:21
  239.6 3.8 collective-permute-done.39
  245.8 6.4 %collective-permute-start.41 = (f32[1,16,64]{2,0,1:T(1,128)S(1)}, f32[1,16,64]{2,0,1:T(1,128)S(1)}, u32[]{:S(2)}, u32[]{:S(2)}) collective-permute-start(f32[1,16,64]{2,0,1:T(1,128)S(1)} %get-tuple-element.239), channel_id=1, source_target_pairs={{16,0},{32,16},{48,32},{64,48},{80,64},{96,80},{112,96},{128,112},... | collective-permute-start | bytes 12296 | tf_op jit(solution)/shard_map/ppermute | solution.py:24
  258.0 3.9 %collective-permute-done.43 = f32[6,1,64]{2,0,1:T(8,128)S(1)} collective-permute-done((f32[6,1,64]{2,0,1:T(8,128)S(1)}, f32[6,1,64]{2,0,1:T(8,128)S(1)}, u32[]{:S(2)}, u32[]{:S(2)}) %collective-permute-start.43) | collective-permute-done | bytes 1568 | tf_op jit(solution)/shard_map/ppermute | solution.py:24
  262.3 5.2 %collective-permute-start.44 = (f32[1,16,64]{2,0,1:T(1,128)S(1)}, f32[1,16,64]{2,0,1:T(1,128)S(1)}, u32[]{:S(2)}, u32[]{:S(2)}) collective-permute-start(f32[1,16,64]{2,0,1:T(1,128)S(1)} %get-tuple-element.236), channel_id=1, source_target_pairs={{0,16},{16,32},{32,48},{48,64},{64,80},{80,96},{96,112},{112,128},... | collective-permute-start | bytes 12296 | tf_op jit(solution)/shard_map/ppermute | solution.py:21
  267.5 3.6 collective-permute-start.45
  278.1 3.9 %collective-permute-done.47 = f32[6,1,64]{2,0,1:T(8,128)S(1)} collective-permute-done((f32[6,1,64]{2,0,1:T(8,128)S(1)}, f32[6,1,64]{2,0,1:T(8,128)S(1)}, u32[]{:S(2)}, u32[]{:S(2)}) %collective-permute-start.47) | collective-permute-done | bytes 1568 | tf_op jit(solution)/shard_map/ppermute | solution.py:24
  285.8 4.9 %collective-permute-start.49 = (f32[1,16,64]{2,0,1:T(1,128)S(1)}, f32[1,16,64]{2,0,1:T(1,128)S(1)}, u32[]{:S(2)}, u32[]{:S(2)}) collective-permute-start(f32[1,16,64]{2,0,1:T(1,128)S(1)} %get-tuple-element.235), channel_id=1, source_target_pairs={{16,0},{32,16},{48,32},{64,48},{80,64},{96,80},{112,96},{128,112},... | collective-permute-start | bytes 12296 | tf_op jit(solution)/shard_map/ppermute | solution.py:24
  296.6 3.9 %collective-permute-done.51 = f32[6,1,64]{2,0,1:T(8,128)S(1)} collective-permute-done((f32[6,1,64]{2,0,1:T(8,128)S(1)}, f32[6,1,64]{2,0,1:T(8,128)S(1)}, u32[]{:S(2)}, u32[]{:S(2)}) %collective-permute-start.51) | collective-permute-done | bytes 1568 | tf_op jit(solution)/shard_map/ppermute | solution.py:24
  300.9 5.6 %collective-permute-start.52 = (f32[1,16,64]{2,0,1:T(1,128)S(1)}, f32[1,16,64]{2,0,1:T(1,128)S(1)}, u32[]{:S(2)}, u32[]{:S(2)}) collective-permute-start(f32[1,16,64]{2,0,1:T(1,128)S(1)} %get-tuple-element.232), channel_id=1, source_target_pairs={{0,16},{16,32},{32,48},{48,64},{64,80},{80,96},{96,112},{112,128},... | collective-permute-start | bytes 12296 | tf_op jit(solution)/shard_map/ppermute | solution.py:21
  317.1 3.9 %collective-permute-done.55 = f32[6,1,64]{2,0,1:T(8,128)S(1)} collective-permute-done((f32[6,1,64]{2,0,1:T(8,128)S(1)}, f32[6,1,64]{2,0,1:T(8,128)S(1)}, u32[]{:S(2)}, u32[]{:S(2)}) %collective-permute-start.55) | collective-permute-done | bytes 1568 | tf_op jit(solution)/shard_map/ppermute | solution.py:24
  321.4 3.8 collective-permute-start.56
  325.2 4.5 %collective-permute-start.57 = (f32[1,16,64]{2,0,1:T(1,128)S(1)}, f32[1,16,64]{2,0,1:T(1,128)S(1)}, u32[]{:S(2)}, u32[]{:S(2)}) collective-permute-start(f32[1,16,64]{2,0,1:T(1,128)S(1)} %get-tuple-element.231), channel_id=1, source_target_pairs={{16,0},{32,16},{48,32},{64,48},{80,64},{96,80},{112,96},{128,112},... | collective-permute-start | bytes 12296 | tf_op jit(solution)/shard_map/ppermute | solution.py:24
  335.8 3.9 %collective-permute-done.59 = f32[6,1,64]{2,0,1:T(8,128)S(1)} collective-permute-done((f32[6,1,64]{2,0,1:T(8,128)S(1)}, f32[6,1,64]{2,0,1:T(8,128)S(1)}, u32[]{:S(2)}, u32[]{:S(2)}) %collective-permute-start.59) | collective-permute-done | bytes 1568 | tf_op jit(solution)/shard_map/ppermute | solution.py:24
  340.1 3.8 collective-permute-start.60
  343.9 4.8 %collective-permute-start.61 = (f32[1,16,64]{2,0,1:T(1,128)S(1)}, f32[1,16,64]{2,0,1:T(1,128)S(1)}, u32[]{:S(2)}, u32[]{:S(2)}) collective-permute-start(f32[1,16,64]{2,0,1:T(1,128)S(1)} %get-tuple-element.229), channel_id=1, source_target_pairs={{16,0},{32,16},{48,32},{64,48},{80,64},{96,80},{112,96},{128,112},... | collective-permute-start | bytes 12296 | tf_op jit(solution)/shard_map/ppermute | solution.py:24
  354.5 3.9 %collective-permute-done.63 = f32[6,1,64]{2,0,1:T(8,128)S(1)} collective-permute-done((f32[6,1,64]{2,0,1:T(8,128)S(1)}, f32[6,1,64]{2,0,1:T(8,128)S(1)}, u32[]{:S(2)}, u32[]{:S(2)}) %collective-permute-start.63) | collective-permute-done | bytes 1568 | tf_op jit(solution)/shard_map/ppermute | solution.py:24
  358.8 6.7 %collective-permute-start.64 = (f32[1,16,64]{2,0,1:T(1,128)S(1)}, f32[1,16,64]{2,0,1:T(1,128)S(1)}, u32[]{:S(2)}, u32[]{:S(2)}) collective-permute-start(f32[1,16,64]{2,0,1:T(1,128)S(1)} %slice.1511), channel_id=1, source_target_pairs={{16,0},{32,16},{48,32},{64,48},{80,64},{96,80},{112,96},{128,112},... | collective-permute-start | bytes 12296 | tf_op jit(solution)/shard_map/ppermute | solution.py:32
  368.2 3.9 %collective-permute-done.65 = f32[5,1,64]{2,0,1:T(8,128)S(1)} collective-permute-done((f32[5,1,64]{2,0,1:T(8,128)S(1)}, f32[5,1,64]{2,0,1:T(8,128)S(1)}, u32[]{:S(2)}, u32[]{:S(2)}) %collective-permute-start.65) | collective-permute-done | bytes 1312 | tf_op jit(solution)/shard_map/ppermute | solution.py:32
  374.6 6.6 %collective-permute-start.66 = (f32[1,32,128]{2,0,1:T(1,128)S(1)}, f32[1,32,128]{2,0,1:T(1,128)S(1)}, u32[]{:S(2)}, u32[]{:S(2)}) collective-permute-start(f32[1,32,128]{2,0,1:T(1,128)S(1)} %slice.1517), channel_id=1, source_target_pairs={{16,0},{32,16},{48,32},{64,48},{80,64},{96,80},{112,96},{128,112},... | collective-permute-start | bytes 49160 | tf_op jit(solution)/shard_map/ppermute | solution.py:32
  383.4 3.8 collective-permute-done.67
  (339 shorter events, 153.8 us)
Async XLA Ops:
  1.3 10.2 %collective-permute-start = (f32[3,1,32,128]{3,1,2,0:T(1,128)S(1)}, f32[3,1,32,128]{3,1,2,0:T(1,128)S(1)}, u32[]{:S(2)}, u32[]{:S(2)}) collective-permute-start(f32[3,1,32,128]{3,1,2,0:T(1,128)S(1)} %get-tuple-element.124), channel_id=1, source_target_pairs={{0,16},{16,32},{32,48},{48,64},{64,80},{80,96},{96,112},{112,128},... | collective-permute-start | bytes 147464 | tf_op jit(solution)/shard_map/ppermute | solution.py:21
  6.2 6.8 %collective-permute-start.1 = (f32[3,1,32,128]{3,1,2,0:T(1,128)S(1)}, f32[3,1,32,128]{3,1,2,0:T(1,128)S(1)}, u32[]{:S(2)}, u32[]{:S(2)}) collective-permute-start(f32[3,1,32,128]{3,1,2,0:T(1,128)S(1)} %get-tuple-element.125), channel_id=1, source_target_pairs={{16,0},{32,16},{48,32},{64,48},{80,64},{96,80},{112,96},{128,112},... | collective-permute-start | bytes 147464 | tf_op jit(solution)/shard_map/ppermute | solution.py:24
  13.0 7.5 %collective-permute-start.2 = (f32[3,10,1,128]{3,1,2,0:T(8,128)S(1)}, f32[3,10,1,128]{3,1,2,0:T(8,128)S(1)}, u32[]{:S(2)}, u32[]{:S(2)}) collective-permute-start(f32[3,10,1,128]{3,1,2,0:T(8,128)S(1)} %get-tuple-element.116), channel_id=1, source_target_pairs={{0,1},{1,2},{2,3},{3,4},{4,5},{5,6},{6,7},{7,8},{8,9},{9,10},{10,1... | collective-permute-start | bytes 46088 | tf_op jit(solution)/shard_map/ppermute | solution.py:21
  18.4 6.0 %collective-permute-start.3 = (f32[3,10,1,128]{3,1,2,0:T(8,128)S(1)}, f32[3,10,1,128]{3,1,2,0:T(8,128)S(1)}, u32[]{:S(2)}, u32[]{:S(2)}) collective-permute-start(f32[3,10,1,128]{3,1,2,0:T(8,128)S(1)} %get-tuple-element.117), channel_id=1, source_target_pairs={{1,0},{2,1},{3,2},{4,3},{5,4},{6,5},{7,6},{8,7},{9,8},{10,9},{11,1... | collective-permute-start | bytes 46088 | tf_op jit(solution)/shard_map/ppermute | solution.py:24
  26.8 8.3 %collective-permute-start.4 = (f32[3,1,32,128]{3,1,2,0:T(1,128)S(1)}, f32[3,1,32,128]{3,1,2,0:T(1,128)S(1)}, u32[]{:S(2)}, u32[]{:S(2)}) collective-permute-start(f32[3,1,32,128]{3,1,2,0:T(1,128)S(1)} %get-tuple-element.122), channel_id=1, source_target_pairs={{0,16},{16,32},{32,48},{48,64},{64,80},{80,96},{96,112},{112,128},... | collective-permute-start | bytes 147464 | tf_op jit(solution)/shard_map/ppermute | solution.py:21
  33.1 5.7 %collective-permute-start.5 = (f32[3,1,32,128]{3,1,2,0:T(1,128)S(1)}, f32[3,1,32,128]{3,1,2,0:T(1,128)S(1)}, u32[]{:S(2)}, u32[]{:S(2)}) collective-permute-start(f32[3,1,32,128]{3,1,2,0:T(1,128)S(1)} %get-tuple-element.123), channel_id=1, source_target_pairs={{16,0},{32,16},{48,32},{64,48},{80,64},{96,80},{112,96},{128,112},... | collective-permute-start | bytes 147464 | tf_op jit(solution)/shard_map/ppermute | solution.py:24
  42.2 6.0 %collective-permute-start.7 = (f32[3,10,1,128]{3,1,2,0:T(8,128)S(1)}, f32[3,10,1,128]{3,1,2,0:T(8,128)S(1)}, u32[]{:S(2)}, u32[]{:S(2)}) collective-permute-start(f32[3,10,1,128]{3,1,2,0:T(8,128)S(1)} %get-tuple-element.115), channel_id=1, source_target_pairs={{1,0},{2,1},{3,2},{4,3},{5,4},{6,5},{7,6},{8,7},{9,8},{10,9},{11,1... | collective-permute-start | bytes 46088 | tf_op jit(solution)/shard_map/ppermute | solution.py:24
  50.2 8.3 %collective-permute-start.8 = (f32[3,1,32,128]{3,1,2,0:T(1,128)S(1)}, f32[3,1,32,128]{3,1,2,0:T(1,128)S(1)}, u32[]{:S(2)}, u32[]{:S(2)}) collective-permute-start(f32[3,1,32,128]{3,1,2,0:T(1,128)S(1)} %get-tuple-element.120), channel_id=1, source_target_pairs={{0,16},{16,32},{32,48},{48,64},{64,80},{80,96},{96,112},{112,128},... | collective-permute-start | bytes 147464 | tf_op jit(solution)/shard_map/ppermute | solution.py:21
  53.3 6.3 %collective-permute-start.9 = (f32[3,1,32,128]{3,1,2,0:T(1,128)S(1)}, f32[3,1,32,128]{3,1,2,0:T(1,128)S(1)}, u32[]{:S(2)}, u32[]{:S(2)}) collective-permute-start(f32[3,1,32,128]{3,1,2,0:T(1,128)S(1)} %get-tuple-element.121), channel_id=1, source_target_pairs={{16,0},{32,16},{48,32},{64,48},{80,64},{96,80},{112,96},{128,112},... | collective-permute-start | bytes 147464 | tf_op jit(solution)/shard_map/ppermute | solution.py:24
  62.7 6.0 %collective-permute-start.11 = (f32[3,10,1,128]{3,1,2,0:T(8,128)S(1)}, f32[3,10,1,128]{3,1,2,0:T(8,128)S(1)}, u32[]{:S(2)}, u32[]{:S(2)}) collective-permute-start(f32[3,10,1,128]{3,1,2,0:T(8,128)S(1)} %get-tuple-element.113), channel_id=1, source_target_pairs={{1,0},{2,1},{3,2},{4,3},{5,4},{6,5},{7,6},{8,7},{9,8},{10,9},{11,1... | collective-permute-start | bytes 46088 | tf_op jit(solution)/shard_map/ppermute | solution.py:24
  70.4 8.9 %collective-permute-start.12 = (f32[3,1,32,128]{3,1,2,0:T(1,128)S(1)}, f32[3,1,32,128]{3,1,2,0:T(1,128)S(1)}, u32[]{:S(2)}, u32[]{:S(2)}) collective-permute-start(f32[3,1,32,128]{3,1,2,0:T(1,128)S(1)} %get-tuple-element.118), channel_id=1, source_target_pairs={{0,16},{16,32},{32,48},{48,64},{64,80},{80,96},{96,112},{112,128},... | collective-permute-start | bytes 147464 | tf_op jit(solution)/shard_map/ppermute | solution.py:21
  74.0 6.5 %collective-permute-start.13 = (f32[3,1,32,128]{3,1,2,0:T(1,128)S(1)}, f32[3,1,32,128]{3,1,2,0:T(1,128)S(1)}, u32[]{:S(2)}, u32[]{:S(2)}) collective-permute-start(f32[3,1,32,128]{3,1,2,0:T(1,128)S(1)} %get-tuple-element.119), channel_id=1, source_target_pairs={{16,0},{32,16},{48,32},{64,48},{80,64},{96,80},{112,96},{128,112},... | collective-permute-start | bytes 147464 | tf_op jit(solution)/shard_map/ppermute | solution.py:24
  83.3 6.0 %collective-permute-start.15 = (f32[3,10,1,128]{3,1,2,0:T(8,128)S(1)}, f32[3,10,1,128]{3,1,2,0:T(8,128)S(1)}, u32[]{:S(2)}, u32[]{:S(2)}) collective-permute-start(f32[3,10,1,128]{3,1,2,0:T(8,128)S(1)} %get-tuple-element.111), channel_id=1, source_target_pairs={{1,0},{2,1},{3,2},{4,3},{5,4},{6,5},{7,6},{8,7},{9,8},{10,9},{11,1... | collective-permute-start | bytes 46088 | tf_op jit(solution)/shard_map/ppermute | solution.py:24
  91.0 9.4 %collective-permute-start.16 = (f32[4,2,32,128]{3,1,2,0:T(2,128)S(1)}, f32[4,2,32,128]{3,1,2,0:T(2,128)S(1)}, u32[]{:S(2)}, u32[]{:S(2)}) collective-permute-start(f32[4,2,32,128]{3,1,2,0:T(2,128)S(1)} %pad_maximum_fusion.20), channel_id=1, source_target_pairs={{0,16},{16,32},{32,48},{48,64},{64,80},{80,96},{96,112},{112,128},... | collective-permute-start | bytes 393224 | tf_op jit(solution)/shard_map/ppermute | solution.py:32
  105.4 8.3 %collective-permute-start.18 = (f32[1,32,128]{2,0,1:T(1,128)S(1)}, f32[1,32,128]{2,0,1:T(1,128)S(1)}, u32[]{:S(2)}, u32[]{:S(2)}) collective-permute-start(f32[1,32,128]{2,0,1:T(1,128)S(1)} %get-tuple-element.180), channel_id=1, source_target_pairs={{0,16},{16,32},{32,48},{48,64},{64,80},{80,96},{96,112},{112,128},... | collective-permute-start | bytes 49160 | tf_op jit(solution)/shard_map/ppermute | solution.py:21
  107.9 8.7 %collective-permute-start.19 = (f32[1,32,128]{2,0,1:T(1,128)S(1)}, f32[1,32,128]{2,0,1:T(1,128)S(1)}, u32[]{:S(2)}, u32[]{:S(2)}) collective-permute-start(f32[1,32,128]{2,0,1:T(1,128)S(1)} %get-tuple-element.181), channel_id=1, source_target_pairs={{16,0},{32,16},{48,32},{64,48},{80,64},{96,80},{112,96},{128,112},... | collective-permute-start | bytes 49160 | tf_op jit(solution)/shard_map/ppermute | solution.py:24
  116.6 8.1 %collective-permute-start.20 = (f32[10,1,128]{2,0,1:T(8,128)S(1)}, f32[10,1,128]{2,0,1:T(8,128)S(1)}, u32[]{:S(2)}, u32[]{:S(2)}) collective-permute-start(f32[10,1,128]{2,0,1:T(8,128)S(1)} %get-tuple-element.169), channel_id=1, source_target_pairs={{0,1},{1,2},{2,3},{3,4},{4,5},{5,6},{6,7},{7,8},{8,9},{9,10},{10,1... | collective-permute-start | bytes 15368 | tf_op jit(solution)/shard_map/ppermute | solution.py:21
  122.8 5.9 %collective-permute-start.21 = (f32[10,1,128]{2,0,1:T(8,128)S(1)}, f32[10,1,128]{2,0,1:T(8,128)S(1)}, u32[]{:S(2)}, u32[]{:S(2)}) collective-permute-start(f32[10,1,128]{2,0,1:T(8,128)S(1)} %get-tuple-element.170), channel_id=1, source_target_pairs={{1,0},{2,1},{3,2},{4,3},{5,4},{6,5},{7,6},{8,7},{9,8},{10,9},{11,1... | collective-permute-start | bytes 15368 | tf_op jit(solution)/shard_map/ppermute | solution.py:24
  129.3 8.3 %collective-permute-start.22 = (f32[1,32,128]{2,0,1:T(1,128)S(1)}, f32[1,32,128]{2,0,1:T(1,128)S(1)}, u32[]{:S(2)}, u32[]{:S(2)}) collective-permute-start(f32[1,32,128]{2,0,1:T(1,128)S(1)} %get-tuple-element.178), channel_id=1, source_target_pairs={{0,16},{16,32},{32,48},{48,64},{64,80},{80,96},{96,112},{112,128},... | collective-permute-start | bytes 49160 | tf_op jit(solution)/shard_map/ppermute | solution.py:21
  143.8 5.9 %collective-permute-start.25 = (f32[10,1,128]{2,0,1:T(8,128)S(1)}, f32[10,1,128]{2,0,1:T(8,128)S(1)}, u32[]{:S(2)}, u32[]{:S(2)}) collective-permute-start(f32[10,1,128]{2,0,1:T(8,128)S(1)} %get-tuple-element.168), channel_id=1, source_target_pairs={{1,0},{2,1},{3,2},{4,3},{5,4},{6,5},{7,6},{8,7},{9,8},{10,9},{11,1... | collective-permute-start | bytes 15368 | tf_op jit(solution)/shard_map/ppermute | solution.py:24
  150.4 8.3 %collective-permute-start.26 = (f32[1,32,128]{2,0,1:T(1,128)S(1)}, f32[1,32,128]{2,0,1:T(1,128)S(1)}, u32[]{:S(2)}, u32[]{:S(2)}) collective-permute-start(f32[1,32,128]{2,0,1:T(1,128)S(1)} %get-tuple-element.176), channel_id=1, source_target_pairs={{0,16},{16,32},{32,48},{48,64},{64,80},{80,96},{96,112},{112,128},... | collective-permute-start | bytes 49160 | tf_op jit(solution)/shard_map/ppermute | solution.py:21
  153.2 6.3 %collective-permute-start.27 = (f32[1,32,128]{2,0,1:T(1,128)S(1)}, f32[1,32,128]{2,0,1:T(1,128)S(1)}, u32[]{:S(2)}, u32[]{:S(2)}) collective-permute-start(f32[1,32,128]{2,0,1:T(1,128)S(1)} %get-tuple-element.177), channel_id=1, source_target_pairs={{16,0},{32,16},{48,32},{64,48},{80,64},{96,80},{112,96},{128,112},... | collective-permute-start | bytes 49160 | tf_op jit(solution)/shard_map/ppermute | solution.py:24
  162.6 5.9 %collective-permute-start.29 = (f32[10,1,128]{2,0,1:T(8,128)S(1)}, f32[10,1,128]{2,0,1:T(8,128)S(1)}, u32[]{:S(2)}, u32[]{:S(2)}) collective-permute-start(f32[10,1,128]{2,0,1:T(8,128)S(1)} %get-tuple-element.166), channel_id=1, source_target_pairs={{1,0},{2,1},{3,2},{4,3},{5,4},{6,5},{7,6},{8,7},{9,8},{10,9},{11,1... | collective-permute-start | bytes 15368 | tf_op jit(solution)/shard_map/ppermute | solution.py:24
  169.2 8.9 %collective-permute-start.30 = (f32[1,32,128]{2,0,1:T(1,128)S(1)}, f32[1,32,128]{2,0,1:T(1,128)S(1)}, u32[]{:S(2)}, u32[]{:S(2)}) collective-permute-start(f32[1,32,128]{2,0,1:T(1,128)S(1)} %get-tuple-element.174), channel_id=1, source_target_pairs={{0,16},{16,32},{32,48},{48,64},{64,80},{80,96},{96,112},{112,128},... | collective-permute-start | bytes 49160 | tf_op jit(solution)/shard_map/ppermute | solution.py:21
  172.5 6.4 %collective-permute-start.31 = (f32[1,32,128]{2,0,1:T(1,128)S(1)}, f32[1,32,128]{2,0,1:T(1,128)S(1)}, u32[]{:S(2)}, u32[]{:S(2)}) collective-permute-start(f32[1,32,128]{2,0,1:T(1,128)S(1)} %get-tuple-element.175), channel_id=1, source_target_pairs={{16,0},{32,16},{48,32},{64,48},{80,64},{96,80},{112,96},{128,112},... | collective-permute-start | bytes 49160 | tf_op jit(solution)/shard_map/ppermute | solution.py:24
  181.7 5.9 %collective-permute-start.33 = (f32[10,1,128]{2,0,1:T(8,128)S(1)}, f32[10,1,128]{2,0,1:T(8,128)S(1)}, u32[]{:S(2)}, u32[]{:S(2)}) collective-permute-start(f32[10,1,128]{2,0,1:T(8,128)S(1)} %get-tuple-element.164), channel_id=1, source_target_pairs={{1,0},{2,1},{3,2},{4,3},{5,4},{6,5},{7,6},{8,7},{9,8},{10,9},{11,1... | collective-permute-start | bytes 15368 | tf_op jit(solution)/shard_map/ppermute | solution.py:24
  193.1 8.1 %collective-permute-start.34 = (f32[1,32,64]{2,0,1:T(1,128)S(1)}, f32[1,32,64]{2,0,1:T(1,128)S(1)}, u32[]{:S(2)}, u32[]{:S(2)}) collective-permute-start(f32[1,32,64]{2,0,1:T(1,128)S(1)} %slice.1415), channel_id=1, source_target_pairs={{0,16},{16,32},{32,48},{48,64},{64,80},{80,96},{96,112},{112,128},... | collective-permute-start | bytes 24584 | tf_op jit(solution)/shard_map/ppermute | solution.py:32
  205.8 26.1 %collective-permute-start.36 = (f32[1,16,64]{2,0,1:T(1,128)S(1)}, f32[1,16,64]{2,0,1:T(1,128)S(1)}, u32[]{:S(2)}, u32[]{:S(2)}) collective-permute-start(f32[1,16,64]{2,0,1:T(1,128)S(1)} %get-tuple-element.240), channel_id=1, source_target_pairs={{0,16},{16,32},{32,48},{48,64},{64,80},{80,96},{96,112},{112,128},... | collective-permute-start | bytes 12296 | tf_op jit(solution)/shard_map/ppermute | solution.py:21
  208.3 23.6 %collective-permute-start.37 = (f32[1,16,64]{2,0,1:T(1,128)S(1)}, f32[1,16,64]{2,0,1:T(1,128)S(1)}, u32[]{:S(2)}, u32[]{:S(2)}) collective-permute-start(f32[1,16,64]{2,0,1:T(1,128)S(1)} %get-tuple-element.241), channel_id=1, source_target_pairs={{16,0},{32,16},{48,32},{64,48},{80,64},{96,80},{112,96},{128,112},... | collective-permute-start | bytes 12296 | tf_op jit(solution)/shard_map/ppermute | solution.py:24
  232.0 7.6 %collective-permute-start.38 = (f32[6,1,64]{2,0,1:T(8,128)S(1)}, f32[6,1,64]{2,0,1:T(8,128)S(1)}, u32[]{:S(2)}, u32[]{:S(2)}) collective-permute-start(f32[6,1,64]{2,0,1:T(8,128)S(1)} %get-tuple-element.226), channel_id=1, source_target_pairs={{0,1},{1,2},{2,3},{3,4},{4,5},{5,6},{6,7},{7,8},{8,9},{9,10},{10,1... | collective-permute-start | bytes 4616 | tf_op jit(solution)/shard_map/ppermute | solution.py:21
  237.6 5.8 %collective-permute-start.39 = (f32[6,1,64]{2,0,1:T(8,128)S(1)}, f32[6,1,64]{2,0,1:T(8,128)S(1)}, u32[]{:S(2)}, u32[]{:S(2)}) collective-permute-start(f32[6,1,64]{2,0,1:T(8,128)S(1)} %get-tuple-element.227), channel_id=1, source_target_pairs={{1,0},{2,1},{3,2},{4,3},{5,4},{6,5},{7,6},{8,7},{9,8},{10,9},{11,1... | collective-permute-start | bytes 4616 | tf_op jit(solution)/shard_map/ppermute | solution.py:24
  243.9 8.3 %collective-permute-start.40 = (f32[1,16,64]{2,0,1:T(1,128)S(1)}, f32[1,16,64]{2,0,1:T(1,128)S(1)}, u32[]{:S(2)}, u32[]{:S(2)}) collective-permute-start(f32[1,16,64]{2,0,1:T(1,128)S(1)} %get-tuple-element.238), channel_id=1, source_target_pairs={{0,16},{16,32},{32,48},{48,64},{64,80},{80,96},{96,112},{112,128},... | collective-permute-start | bytes 12296 | tf_op jit(solution)/shard_map/ppermute | solution.py:21
  245.8 7.1 %collective-permute-start.41 = (f32[1,16,64]{2,0,1:T(1,128)S(1)}, f32[1,16,64]{2,0,1:T(1,128)S(1)}, u32[]{:S(2)}, u32[]{:S(2)}) collective-permute-start(f32[1,16,64]{2,0,1:T(1,128)S(1)} %get-tuple-element.239), channel_id=1, source_target_pairs={{16,0},{32,16},{48,32},{64,48},{80,64},{96,80},{112,96},{128,112},... | collective-permute-start | bytes 12296 | tf_op jit(solution)/shard_map/ppermute | solution.py:24
  256.0 5.8 %collective-permute-start.43 = (f32[6,1,64]{2,0,1:T(8,128)S(1)}, f32[6,1,64]{2,0,1:T(8,128)S(1)}, u32[]{:S(2)}, u32[]{:S(2)}) collective-permute-start(f32[6,1,64]{2,0,1:T(8,128)S(1)} %get-tuple-element.225), channel_id=1, source_target_pairs={{1,0},{2,1},{3,2},{4,3},{5,4},{6,5},{7,6},{8,7},{9,8},{10,9},{11,1... | collective-permute-start | bytes 4616 | tf_op jit(solution)/shard_map/ppermute | solution.py:24
  262.3 8.9 %collective-permute-start.44 = (f32[1,16,64]{2,0,1:T(1,128)S(1)}, f32[1,16,64]{2,0,1:T(1,128)S(1)}, u32[]{:S(2)}, u32[]{:S(2)}) collective-permute-start(f32[1,16,64]{2,0,1:T(1,128)S(1)} %get-tuple-element.236), channel_id=1, source_target_pairs={{0,16},{16,32},{32,48},{48,64},{64,80},{80,96},{96,112},{112,128},... | collective-permute-start | bytes 12296 | tf_op jit(solution)/shard_map/ppermute | solution.py:21
  276.2 5.8 %collective-permute-start.47 = (f32[6,1,64]{2,0,1:T(8,128)S(1)}, f32[6,1,64]{2,0,1:T(8,128)S(1)}, u32[]{:S(2)}, u32[]{:S(2)}) collective-permute-start(f32[6,1,64]{2,0,1:T(8,128)S(1)} %get-tuple-element.223), channel_id=1, source_target_pairs={{1,0},{2,1},{3,2},{4,3},{5,4},{6,5},{7,6},{8,7},{9,8},{10,9},{11,1... | collective-permute-start | bytes 4616 | tf_op jit(solution)/shard_map/ppermute | solution.py:24
  282.4 8.3 %collective-permute-start.48 = (f32[1,16,64]{2,0,1:T(1,128)S(1)}, f32[1,16,64]{2,0,1:T(1,128)S(1)}, u32[]{:S(2)}, u32[]{:S(2)}) collective-permute-start(f32[1,16,64]{2,0,1:T(1,128)S(1)} %get-tuple-element.234), channel_id=1, source_target_pairs={{0,16},{16,32},{32,48},{48,64},{64,80},{80,96},{96,112},{112,128},... | collective-permute-start | bytes 12296 | tf_op jit(solution)/shard_map/ppermute | solution.py:21
  294.6 5.8 %collective-permute-start.51 = (f32[6,1,64]{2,0,1:T(8,128)S(1)}, f32[6,1,64]{2,0,1:T(8,128)S(1)}, u32[]{:S(2)}, u32[]{:S(2)}) collective-permute-start(f32[6,1,64]{2,0,1:T(8,128)S(1)} %get-tuple-element.221), channel_id=1, source_target_pairs={{1,0},{2,1},{3,2},{4,3},{5,4},{6,5},{7,6},{8,7},{9,8},{10,9},{11,1... | collective-permute-start | bytes 4616 | tf_op jit(solution)/shard_map/ppermute | solution.py:24
  300.9 8.9 %collective-permute-start.52 = (f32[1,16,64]{2,0,1:T(1,128)S(1)}, f32[1,16,64]{2,0,1:T(1,128)S(1)}, u32[]{:S(2)}, u32[]{:S(2)}) collective-permute-start(f32[1,16,64]{2,0,1:T(1,128)S(1)} %get-tuple-element.232), channel_id=1, source_target_pairs={{0,16},{16,32},{32,48},{48,64},{64,80},{80,96},{96,112},{112,128},... | collective-permute-start | bytes 12296 | tf_op jit(solution)/shard_map/ppermute | solution.py:21
  315.2 5.8 %collective-permute-start.55 = (f32[6,1,64]{2,0,1:T(8,128)S(1)}, f32[6,1,64]{2,0,1:T(8,128)S(1)}, u32[]{:S(2)}, u32[]{:S(2)}) collective-permute-start(f32[6,1,64]{2,0,1:T(8,128)S(1)} %get-tuple-element.219), channel_id=1, source_target_pairs={{1,0},{2,1},{3,2},{4,3},{5,4},{6,5},{7,6},{8,7},{9,8},{10,9},{11,1... | collective-permute-start | bytes 4616 | tf_op jit(solution)/shard_map/ppermute | solution.py:24
  321.4 8.3 %collective-permute-start.56 = (f32[1,16,64]{2,0,1:T(1,128)S(1)}, f32[1,16,64]{2,0,1:T(1,128)S(1)}, u32[]{:S(2)}, u32[]{:S(2)}) collective-permute-start(f32[1,16,64]{2,0,1:T(1,128)S(1)} %get-tuple-element.230), channel_id=1, source_target_pairs={{0,16},{16,32},{32,48},{48,64},{64,80},{80,96},{96,112},{112,128},... | collective-permute-start | bytes 12296 | tf_op jit(solution)/shard_map/ppermute | solution.py:21
  333.9 5.8 %collective-permute-start.59 = (f32[6,1,64]{2,0,1:T(8,128)S(1)}, f32[6,1,64]{2,0,1:T(8,128)S(1)}, u32[]{:S(2)}, u32[]{:S(2)}) collective-permute-start(f32[6,1,64]{2,0,1:T(8,128)S(1)} %get-tuple-element.217), channel_id=1, source_target_pairs={{1,0},{2,1},{3,2},{4,3},{5,4},{6,5},{7,6},{8,7},{9,8},{10,9},{11,1... | collective-permute-start | bytes 4616 | tf_op jit(solution)/shard_map/ppermute | solution.py:24
  340.1 8.6 %collective-permute-start.60 = (f32[1,16,64]{2,0,1:T(1,128)S(1)}, f32[1,16,64]{2,0,1:T(1,128)S(1)}, u32[]{:S(2)}, u32[]{:S(2)}) collective-permute-start(f32[1,16,64]{2,0,1:T(1,128)S(1)} %get-tuple-element.228), channel_id=1, source_target_pairs={{0,16},{16,32},{32,48},{48,64},{64,80},{80,96},{96,112},{112,128},... | collective-permute-start | bytes 12296 | tf_op jit(solution)/shard_map/ppermute | solution.py:21
  352.6 5.8 %collective-permute-start.63 = (f32[6,1,64]{2,0,1:T(8,128)S(1)}, f32[6,1,64]{2,0,1:T(8,128)S(1)}, u32[]{:S(2)}, u32[]{:S(2)}) collective-permute-start(f32[6,1,64]{2,0,1:T(8,128)S(1)} %get-tuple-element.215), channel_id=1, source_target_pairs={{1,0},{2,1},{3,2},{4,3},{5,4},{6,5},{7,6},{8,7},{9,8},{10,9},{11,1... | collective-permute-start | bytes 4616 | tf_op jit(solution)/shard_map/ppermute | solution.py:24
  358.8 7.4 %collective-permute-start.64 = (f32[1,16,64]{2,0,1:T(1,128)S(1)}, f32[1,16,64]{2,0,1:T(1,128)S(1)}, u32[]{:S(2)}, u32[]{:S(2)}) collective-permute-start(f32[1,16,64]{2,0,1:T(1,128)S(1)} %slice.1511), channel_id=1, source_target_pairs={{16,0},{32,16},{48,32},{64,48},{80,64},{96,80},{112,96},{128,112},... | collective-permute-start | bytes 12296 | tf_op jit(solution)/shard_map/ppermute | solution.py:32
  366.3 5.8 %collective-permute-start.65 = (f32[5,1,64]{2,0,1:T(8,128)S(1)}, f32[5,1,64]{2,0,1:T(8,128)S(1)}, u32[]{:S(2)}, u32[]{:S(2)}) collective-permute-start(f32[5,1,64]{2,0,1:T(8,128)S(1)} %pad_maximum_fusion.58), channel_id=1, source_target_pairs={{1,0},{2,1},{3,2},{4,3},{5,4},{6,5},{7,6},{8,7},{9,8},{10,9},{11,1... | collective-permute-start | bytes 3848 | tf_op jit(solution)/shard_map/ppermute | solution.py:32
  374.6 12.5 %collective-permute-start.66 = (f32[1,32,128]{2,0,1:T(1,128)S(1)}, f32[1,32,128]{2,0,1:T(1,128)S(1)}, u32[]{:S(2)}, u32[]{:S(2)}) collective-permute-start(f32[1,32,128]{2,0,1:T(1,128)S(1)} %slice.1517), channel_id=1, source_target_pairs={{16,0},{32,16},{48,32},{64,48},{80,64},{96,80},{112,96},{128,112},... | collective-permute-start | bytes 49160 | tf_op jit(solution)/shard_map/ppermute | solution.py:32
  381.3 5.8 %collective-permute-start.67 = (f32[8,1,128]{2,0,1:T(8,128)S(1)}, f32[8,1,128]{2,0,1:T(8,128)S(1)}, u32[]{:S(2)}, u32[]{:S(2)}) collective-permute-start(f32[8,1,128]{2,0,1:T(8,128)S(1)} %slice.1519), channel_id=1, source_target_pairs={{1,0},{2,1},{3,2},{4,3},{5,4},{6,5},{7,6},{8,7},{9,8},{10,9},{11,1... | collective-permute-start | bytes 12296 | tf_op jit(solution)/shard_map/ppermute | solution.py:32
  (21 other events, 103.2 us)
where the time goes:
time: 390 us; the launch traced here: 388 us
  starting transfers between devices  245 us (63%)
  waiting for transfers between devices  98.2 us (25%)
  local copies, waits for them, and re-layouts  26.2 us (7%)
  other arithmetic  17.1 us (4%)
    ppermute x30, starting transfers between devices, with_halo(): lax.ppermute(lax.slice_in_dim(block, block.shape[dim] - width, None, axis...  113 us
    ppermute x30, starting transfers between devices, with_halo(): lax.ppermute(lax.slice_in_dim(block, 0, width, axis=dim), axis, backward)  98.2 us
    ppermute x30, waiting for transfers between devices, with_halo(): lax.ppermute(lax.slice_in_dim(block, 0, width, axis=dim), axis, backward)  80.1 us
    ppermute x8, starting transfers between devices, shifted(): lax.ppermute(value, axis, [(source, source + steps) for source in range(i...  33.2 us
    ppermute x8, waiting for transfers between devices, shifted(): lax.ppermute(value, axis, [(source, source + steps) for source in range(i...  18 us
    another operation x1, local copies, waits for them, and re-layouts, block_mean(): field.reshape(a_len // 2, 2, b_len // 2, 2, c_len // 2, 2)  12.7 us
  transfers between devices with their start and end apart: 68, of which 36 were waited for; matrix products, arithmetic and copies ran while one was open for 5% of the time, Pallas kernels for 0%

commit v1 on v0

v1 whole, which is shorter than its diff:
```python
import functools

import jax
import jax.numpy as jnp
from jax import lax
from jax.experimental import pallas as pl
from jax.experimental.pallas import tpu as pltpu
from jax.sharding import PartitionSpec as P

MESH = pl.DeviceIdType.MESH
ROWS = 48


def coefficients(top, ratio, count):
    low = top / ratio
    center = 0.5 * (top + low)
    radius = 0.5 * (top - low)
    sharp = center / radius
    rho = 1.0 / sharp
    steps = []
    for _ in range(1, count):
        rho_next = 1.0 / (2.0 * sharp - rho)
        steps.append((rho_next * rho, 2.0 * rho_next / radius))
        rho = rho_next
    return 1.0 / center, steps


def roll(value, shift, axis):
    return pltpu.roll(value, shift % value.shape[axis], axis)


def kernel(nx, ny, rhs, classes, table, out, base, kinds, sig, upd, res, acc,
           pack_dn, pack_up, got_dn, got_up, nod, node_sum, red, cs_main, cs_dn, cs_up,
           cf_main, cf_dn, cf_up, cm_one, g_one, g_two, s_one, s_two, fine,
           sem_in, send, recv, far_send, far_recv, x2_send, x2_recv, cs_send, cs_recv, x3_send, x3_recv):
    gx, gy = lax.axis_index("gx"), lax.axis_index("gy")
    first_x, last_x, first_y, last_y = gx == 0, gx == nx - 1, gy == 0, gy == ny - 1

    def at(dx, dy):
        return (lax.rem(gx + dx + nx, nx), lax.rem(gy + dy + ny, ny))

    near = [(1, 0), (-1, 0), (0, 1), (0, -1), (1, 1), (1, -1), (-1, 1), (-1, -1)]
    distant = [(2, 0), (-2, 0), (2, 1), (2, -1), (-2, 1), (-2, -1)]

    def remote(source, target, sems, index, where):
        return pltpu.make_async_remote_copy(
            src_ref=source, dst_ref=target, send_sem=sems[0].at[index], recv_sem=sems[1].at[index],
            device_id=at(*where), device_id_type=MESH)

    barrier = pltpu.get_barrier_semaphore()
    for where in near + distant:
        pl.semaphore_signal(barrier, inc=1, device_id=at(*where), device_id_type=MESH)
    load_rhs = pltpu.make_async_copy(rhs, base.at[:, 3:11, 0:32], sem_in.at[0])
    load_kinds = pltpu.make_async_copy(classes, kinds, sem_in.at[1])
    load_rhs.start()
    load_kinds.start()

    load_kinds.wait()
    values = [table[k] for k in range(16)]
    for x in range(8):
        code = kinds[x]
        level = values
        for bit in range(4):
            flag = (code & (1 << bit)) != 0
            level = [jnp.where(flag, level[2 * i + 1], level[2 * i]) for i in range(len(level) // 2)]
        sig[x + 4, 0:32] = level[0]
    load_rhs.wait()

    pl.semaphore_wait(barrier, len(near + distant))
    x1 = (send, recv)
    first = [
        remote(base.at[:, 8:11, 0:32], base.at[:, 0:3, 0:32], x1, 0, (1, 0)),
        remote(base.at[:, 3:6, 0:32], base.at[:, 11:14, 0:32], x1, 1, (-1, 0)),
    ]
    for copy in first:
        copy.start()

    sub = lax.broadcasted_iota(jnp.int32, (8, 128), 0)
    lower = sub < 4
    for x in range(8):
        ux, uy, uz = (base[c, x + 3, 0:8] for c in range(3))
        sg = sig[x + 4, 0:8]
        pack_dn[x, 0] = jnp.where(lower, ux, roll(uy, 4, 0))
        pack_dn[x, 1] = jnp.where(lower, uz, roll(sg, 4, 0))
        ux, uy, uz = (base[c, x + 3, 24:32] for c in range(3))
        sg = sig[x + 4, 24:32]
        pack_up[x, 0] = jnp.where(lower, roll(uy, 4, 0), ux)
        pack_up[x, 1] = jnp.where(lower, roll(sg, 4, 0), uz)
    for x in range(8):
        pack_up[8, 0, x:x + 1] = sig[x + 4, 27:28]
    pack_up[8, 1] = jnp.zeros((8, 128), jnp.float32)

    second = [
        remote(pack_dn.at[0:3], got_dn.at[12:15], x1, 2, (-1, -1)),
        remote(pack_up.at[0:3], got_up.at[13:16], x1, 3, (-1, 1)),
        remote(pack_dn.at[5:8], got_dn.at[9:12], x1, 4, (1, -1)),
        remote(pack_up.at[4:8], got_up.at[9:13], x1, 5, (1, 1)),
        remote(pack_dn, got_dn.at[0:8], x1, 6, (0, -1)),
        remote(pack_up, got_up.at[0:9], x1, 7, (0, 1)),
        remote(sig.at[10:12, 0:32], sig.at[2:4, 0:32], x1, 8, (1, 0)),
        remote(sig.at[4:6, 0:32], sig.at[12:14, 0:32], x1, 9, (-1, 0)),
    ]
    for copy in second:
        copy.start()
    far = (far_send, far_recv)
    later = [
        remote(sig.at[8:10, 0:32], sig.at[0:2, 0:32], far, 0, (1, 0)),
        remote(sig.at[6:7, 0:32], sig.at[14:15, 0:32], far, 1, (-1, 0)),
    ]
    for copy in later:
        copy.start()

    lane = lax.broadcasted_iota(jnp.int32, (ROWS, 128), 1)
    row = lax.broadcasted_iota(jnp.int32, (ROWS, 128), 0)
    lane_end, lane_start = lane == 127, lane == 0
    f32 = lambda flag: flag.astype(jnp.float32)
    keep_hi, keep_lo = 1.0 - f32(last_y), 1.0 - f32(first_y)
    row_mask = jnp.where(row < 32, 1.0, jnp.where(row < 40, keep_hi, keep_lo))
    row_zero = (row[0:8] == 0) & first_y

    def next_z(f):
        return jnp.where(lane_end, 0.0, roll(f, -1, 1))

    def prev_z(f):
        return jnp.where(lane_start, 0.0, roll(f, 1, 1))

    def next_y(f):
        return roll(f, -1, 0)

    def prev_y(f):
        return roll(f, 1, 0)

    def prev_y_inside(f):
        moved = roll(f, 1, 0)
        return jnp.concatenate([jnp.where(row_zero, 0.0, moved[0:8]), moved[8:]], axis=0)

    fine_z = lax.broadcasted_iota(jnp.int32, (256, 128), 0)
    packed_z = lax.broadcasted_iota(jnp.int32, (256, 128), 1)
    half = fine_z // 128 == packed_z // 64
    apart = (fine_z % 128) - 2 * (packed_z % 64)
    mean_z = jnp.where(half & ((apart == 0) | (apart == 1)), 0.125, 0.0)
    rest_z = jnp.where(half, jnp.where(apart == 0, 1.0, jnp.where(jnp.abs(apart) == 1, 0.5, 0.0)), 0.0)
    dot = functools.partial(jnp.dot, precision=lax.Precision.HIGHEST, preferred_element_type=jnp.float32)

    for x in range(4):
        red[x, 8:40] = sig[2 * x + 4, 0:32] + sig[2 * x + 5, 0:32]
    pairs = [red[x, pl.ds(8, 16, stride=2)] + red[x, pl.ds(9, 16, stride=2)] for x in range(4)]
    wide = jnp.concatenate(
        [jnp.concatenate([p[0:8] for p in pairs], axis=0), jnp.concatenate([p[8:16] for p in pairs], axis=0)], axis=1)
    coarse = 2.0 * dot(wide, mean_z)
    for x in range(4):
        cs_main[7 + x] = coarse[8 * x:8 * x + 8]

    plane_x = lax.broadcasted_iota(jnp.int32, (19, 8, 128), 0) - 7 + 4 * gx
    plane_ok = (plane_x >= 0) & (plane_x < 4 * nx)
    left3 = lax.broadcasted_iota(jnp.int32, (19, 8, 128), 2) < 64
    cm_one[0] = jnp.where(plane_ok, 1.0, 0.0)
    cm_one[1] = jnp.where(plane_ok, jnp.where(left3, keep_hi, keep_lo), 0.0)

    for copy in first + second:
        copy.wait()

    def spot_dn(x):
        return x if 0 <= x < 8 else (12 + x if x < 0 else 4 + x)

    def spot_up(x):
        return x if 0 <= x < 8 else (13 + x if x < 0 else 5 + x)

    zero_tile = jnp.zeros((8, 128), jnp.float32)
    for x in range(-4, 11):
        if x > -4:
            a, b = got_dn[spot_dn(x), 0], got_dn[spot_dn(x), 1]
            base[0, x + 3, 32:40] = a * keep_hi
            base[1, x + 3, 32:40] = roll(a, 4, 0) * keep_hi
            base[2, x + 3, 32:40] = b * keep_hi
            sig[x + 4, 32:40] = roll(b, 4, 0) * keep_hi
        else:
            sig[x + 4, 32:40] = zero_tile
        a, b = got_up[spot_up(x), 0], got_up[spot_up(x), 1]
        if x > -4:
            base[0, x + 3, 40:48] = a * keep_lo
            base[1, x + 3, 40:48] = roll(a, 4, 0) * keep_lo
            base[2, x + 3, 40:48] = b * keep_lo
        sg = roll(b, 4, 0)
        if 0 <= x < 8:
            sg = jnp.where(sub == 3, got_up[8, 0, x:x + 1], sg)
        sig[x + 4, 40:48] = sg * keep_lo

    @pl.when(first_x)
    def _():
        base[:, 0:3] = jnp.zeros((3, 3, ROWS, 128), jnp.float32)
        sig[2:4] = jnp.zeros((2, ROWS, 128), jnp.float32)

    @pl.when(last_x)
    def _():
        base[:, 11:14] = jnp.zeros((3, 3, ROWS, 128), jnp.float32)
        sig[12:14] = jnp.zeros((2, ROWS, 128), jnp.float32)

    keep_left, keep_right = 1.0 - f32(first_x), 1.0 - f32(last_x)

    def side(x):
        return keep_left if x < 0 else (keep_right if x > 7 else None)

    inv, steps = coefficients(20.0, 30.0, 4)
    nodal_prev = None
    for turn, (c_old, c_res) in enumerate(steps):
        lo, hi = -2 + turn, 9 - turn
        get = (lambda c, x: base[c, x + 3]) if turn == 0 else (lambda c, x: upd[c, x + 2])
        scaled = row_mask * c_res
        before = None
        here = [get(c, lo - 1) for c in range(3)]
        for x in range(lo - 1, hi + 1):
            after = [None if (c == 0 and x == hi) else get(c, x + 1) for c in range(3)]
            ux, uy, uz = here
            cy = (next_z(ux) - ux) - (after[2] - uz)
            cz = (after[1] - uy) - (next_y(ux) - ux)
            if x == -1:
                cy, cz = cy * keep_left, cz * keep_left
            if x >= lo:
                cx = (next_y(uz) - uz) - (next_z(uy) - uy)
                sg = sig[x + 4]
                applied = [
                    (prev_y_inside(cz) - cz) - (prev_z(cy) - cy) + sg * ux,
                    (prev_z(cx) - cx) - (before[1] - cz) + sg * uy,
                    (before[0] - cy) - (prev_y_inside(cx) - cx) + sg * uz,
                ]
                weight = scaled if side(x) is None else scaled * side(x)
                left = []
                for c in range(3):
                    if turn == 0:
                        u = here[c] * inv
                        r = here[c] - applied[c] * inv
                    else:
                        u = here[c]
                        r = res[c, x + 2] - applied[c]
                    new = c_old * u + weight * r
                    if turn < 2:
                        upd[c, x + 2] = new
                        res[c, x + 2] = r
                        if 0 <= x < 8:
                            acc[c, x] = u + new if turn == 0 else acc[c, x] + new
                    else:
                        answer = acc[c, x] + new
                        acc[c, x] = answer
                        left.append(base[c, x + 3] - sg * answer)
                if turn == 2:
                    rx, ry, rz = left
                    total = (ry - prev_y(ry)) + (rz - prev_z(rz)) + rx
                    nod[x + 5, 0:32] = (total if nodal_prev is None else total - nodal_prev)[0:32]
                    nodal_prev = rx
                    if x == 7:
                        nod[13, 0:32] = rx[0:32]
            before = (cy, cz)
            here = after

    x2 = (x2_send, x2_recv)
    swap = [
        remote(nod.at[9:14, 0:32], nod.at[0:5, 0:32], x2, 0, (1, 0)),
        remote(nod.at[5:9, 0:32], nod.at[14:18, 0:32], x2, 1, (-1, 0)),
        remote(nod.at[9:14, 24:32], nod.at[0:5, 40:48], x2, 2, (1, 1)),
        remote(nod.at[9:14, 0:8], nod.at[0:5, 32:40], x2, 3, (1, -1)),
        remote(nod.at[5:9, 24:32], nod.at[14:18, 40:48], x2, 4, (-1, 1)),
        remote(nod.at[5:9, 0:8], nod.at[14:18, 32:40], x2, 5, (-1, -1)),
        remote(nod.at[5:14, 24:32], nod.at[5:14, 40:48], x2, 6, (0, 1)),
        remote(nod.at[5:14, 0:8], nod.at[5:14, 32:40], x2, 7, (0, -1)),
    ]
    for copy in swap:
        copy.start()

    csem = (cs_send, cs_recv)

    def spread(main, dn, up, sems, own, count):
        block = main.at[own:own + count]
        span = {1: own - count, -1: own + count}
        copies = []
        for k, dx in enumerate((1, -1)):
            spot = span[dx]
            copies.append(remote(block, main.at[spot:spot + count], sems, 6 * k, (dx, 0)))
            copies.append(remote(block, dn.at[spot:spot + count], sems, 6 * k + 1, (dx, -1)))
            copies.append(remote(block, up.at[spot:spot + count], sems, 6 * k + 2, (dx, 1)))
        far_low, far_high = main.at[own + 1:own + count], main.at[own:own + 4]
        size = count - 1
        end = own + 2 * count
        copies.append(remote(far_low, main.at[0:size], sems, 3, (2, 0)))
        copies.append(remote(far_low, dn.at[0:size], sems, 4, (2, -1)))
        copies.append(remote(far_low, up.at[0:size], sems, 5, (2, 1)))
        copies.append(remote(far_high, main.at[end:end + 4], sems, 9, (-2, 0)))
        copies.append(remote(far_high, dn.at[end:end + 4], sems, 10, (-2, -1)))
        copies.append(remote(far_high, up.at[end:end + 4], sems, 11, (-2, 1)))
        copies.append(remote(block, dn.at[own:own + count], sems, 12, (0, -1)))
        copies.append(remote(block, up.at[own:own + count], sems, 13, (0, 1)))
        return copies

    cs_copies = spread(cs_main, cs_dn, cs_up, csem, 7, 4)
    for copy in cs_copies:
        copy.start()

    for copy in later + swap:
        copy.wait()

    @pl.when(first_x)
    def _():
        nod[0:5] = jnp.zeros((5, ROWS, 128), jnp.float32)
        sig[0:2] = jnp.zeros((2, ROWS, 128), jnp.float32)

    @pl.when(last_x)
    def _():
        sig[14:15] = jnp.zeros((1, ROWS, 128), jnp.float32)

    nod[5] = nod[5] - nod[4]
    nod[14] = nod[14] - nod[13]

    @pl.when(last_x)
    def _():
        nod[14:18] = jnp.zeros((4, ROWS, 128), jnp.float32)

    @pl.when(first_y)
    def _():
        nod[:, 40:48] = jnp.zeros((18, 8, 128), jnp.float32)

    @pl.when(last_y)
    def _():
        nod[:, 32:40] = jnp.zeros((18, 8, 128), jnp.float32)

    def place(x):
        return x + 4 if x < 0 else (x + 5 if x < 8 else x + 6)

    inv, steps = coefficients(48.0, 30.0, 4)
    steps = steps + [None]
    nupd, nres = upd.at[0], res.at[0]
    planes = []
    for turn, step in enumerate(steps):
        lo, hi = -3 + turn, 10 - turn
        get = (lambda x: nod[place(x)]) if turn == 0 else (lambda x: nupd[x + 3])
        here = get(lo - 1)
        before = None
        for x in range(lo - 1, hi + 1):
            after = get(x + 1)
            sg = sig[x + 4]
            flux_x = sg * (after - here)
            if x >= lo:
                flux_y = sg * (next_y(here) - here)
                flux_z = sg * (next_z(here) - here)
                applied = (flux_x - before) + (flux_y - prev_y(flux_y)) + (flux_z - prev_z(flux_z))
                if turn == 0:
                    u = here * inv
                    r = here - applied * inv
                else:
                    u = here
                    r = nres[x + 3] - applied
                if step is not None:
                    weight = row_mask * step[1]
                    weight = weight if side(x) is None else weight * side(x)
                    new = step[0] * u + weight * r
                    nupd[x + 3] = new
                    nres[x + 3] = r
                    if 0 <= x < 9:
                        node_sum[x] = u + new if turn == 0 else node_sum[x] + new
                else:
                    planes.append(r)
                    if x % 2 == 1:
                        total = planes[x - 1] + 0.5 * planes[x]
                        if x > 1:
                            total = total + 0.5 * planes[x - 2]
                        red[x // 2, 8:40] = total[0:32]
                        red[x // 2, 0:8] = total[40:48] * keep_lo
                    if x == 7:
                        red[4, 8:40] = 0.5 * r[0:32]
                        red[4, 0:8] = 0.5 * r[40:48] * keep_lo
            before = flux_x
            here = after

    thin = [red[x, pl.ds(8, 16, stride=2)] + 0.5 * (red[x, pl.ds(9, 16, stride=2)] + red[x, pl.ds(7, 16, stride=2)])
            for x in range(5)]
    wide = jnp.concatenate(
        [jnp.concatenate([p[0:8] for p in thin], axis=0), jnp.concatenate([p[8:16] for p in thin], axis=0)], axis=1)
    coarse = dot(wide, rest_z)
    for x in range(5):
        cf_main[9 + x] = coarse[8 * x:8 * x + 8]
    cf_copies = spread(cf_main, cf_dn, cf_up, (x3_send, x3_recv), 9, 5)
    for copy in cf_copies:
        copy.start()
    for copy in cs_copies:
        copy.wait()

    left = lax.broadcasted_iota(jnp.int32, (8, 128), 1) < 64
    for x in range(19):
        s_one[x] = cs_main[x] * cm_one[0, x]
        s_two[x] = jnp.where(left, cs_dn[x], cs_up[x]) * cm_one[1, x]

    for copy in cf_copies:
        copy.wait()

    def joined(i):
        return cf_main[i], jnp.where(left, cf_dn[i], cf_up[i])

    where_plane = [0, 1, 2, 4, 5, 6, 7, 9, 10, 11, 12, 14, 15, 16, 17, 19, 20, 21, 22]
    extra = {-4: (3, gx > 1), 0: (8, gx > 0), 4: (13, None), 8: (18, None)}
    for x in range(-7, 12):
        one, two = joined(where_plane[x + 7])
        if x in extra:
            spot, valid = extra[x]
            add_one, add_two = joined(spot)
            scale = 1.0 if valid is None else f32(valid)
            one, two = one + scale * add_one, two + scale * add_two
        g_one[x + 7] = one * cm_one[0, x + 7]
        g_two[x + 7] = two * cm_one[1, x + 7]

    inv, steps = coefficients(96.0, 100.0, 8)

    def lanes3(n):
        return lax.broadcasted_iota(jnp.int32, (n, 8, 128), 2)

    def swapped(one, two, first_side):
        turn_one, turn_two = roll(one, 64, 2), roll(two, 64, 2)
        pick = lanes3(one.shape[0]) < 64
        if first_side:
            return jnp.where(pick, turn_one, turn_two), jnp.where(pick, turn_two, turn_one)
        return jnp.where(pick, turn_two, turn_one), jnp.where(pick, turn_one, turn_two)

    def coarse_next_y(one, two):
        seam_one, seam_two = swapped(one, two, True)
        top = lax.broadcasted_iota(jnp.int32, one.shape, 1) == 0
        return roll(jnp.where(top, seam_one, one), -1, 1), roll(jnp.where(top, seam_two, two), -1, 1)

    def coarse_prev_y(one, two):
        seam_one, seam_two = swapped(one, two, False)
        bottom = lax.broadcasted_iota(jnp.int32, one.shape, 1) == 7
        return roll(jnp.where(bottom, seam_one, one), 1, 1), roll(jnp.where(bottom, seam_two, two), 1, 1)

    def coarse_next_z(f):
        return jnp.where(lanes3(f.shape[0]) % 64 == 63, 0.0, roll(f, -1, 2))

    def coarse_prev_z(f):
        return jnp.where(lanes3(f.shape[0]) % 64 == 0, 0.0, roll(f, 1, 2))

    f_one, f_two = g_one[...], g_two[...]
    r_one = r_two = None
    answer = None
    low = -7
    for turn, (c_old, c_res) in enumerate(steps):
        n = f_one.shape[0]
        sg_one, sg_two = s_one[low + 7:low + 7 + n], s_two[low + 7:low + 7 + n]
        x_one = sg_one[:-1] * (f_one[1:] - f_one[:-1])
        x_two = sg_two[:-1] * (f_two[1:] - f_two[:-1])
        mid_one, mid_two = f_one[1:-1], f_two[1:-1]
        in_one, in_two = sg_one[1:-1], sg_two[1:-1]
        up_one, up_two = coarse_next_y(mid_one, mid_two)
        y_one, y_two = in_one * (up_one - mid_one), in_two * (up_two - mid_two)
        back_one, back_two = coarse_prev_y(y_one, y_two)
        results = []
        for f, x_flux, y_flux, y_back, s in (
            (mid_one, x_one, y_one, back_one, in_one), (mid_two, x_two, y_two, back_two, in_two)):
            z_flux = s * (coarse_next_z(f) - f)
            results.append((x_flux[1:] - x_flux[:-1]) + (y_flux - y_back) + (z_flux - coarse_prev_z(z_flux)))
        low += 1
        if turn == 0:
            r_one, r_two = mid_one - results[0] * inv, mid_two - results[1] * inv
            mid_one, mid_two = mid_one * inv, mid_two * inv
            answer = [mid_one[6:11], mid_two[6:11]]
        else:
            r_one, r_two = r_one[1:-1] - results[0], r_two[1:-1] - results[1]
        n -= 2
        f_one = c_old * mid_one + c_res * (cm_one[0, low + 7:low + 7 + n] * r_one)
        f_two = c_old * mid_two + c_res * (cm_one[1, low + 7:low + 7 + n] * r_two)
        answer = [answer[0] + f_one[-low:5 - low], answer[1] + f_two[-low:5 - low]]

    coarse_k = lax.broadcasted_iota(jnp.int32, (128, 256), 0)
    fine_k = lax.broadcasted_iota(jnp.int32, (128, 256), 1)
    same = coarse_k // 64 == fine_k // 128
    apart = (fine_k % 128) - 2 * (coarse_k % 64)
    grow = jnp.where(same, jnp.where(apart == 0, 1.0, jnp.where(jnp.abs(apart) == 1, 0.5, 0.0)), 0.0)
    body = dot(answer[0].reshape(40, 128), grow)
    edge = dot(answer[1].reshape(40, 128), grow[:, 0:128])
    for x in range(5):
        fine[x, 0:8] = body[8 * x:8 * x + 8, 0:128]
        fine[x, 8:16] = body[8 * x:8 * x + 8, 128:256]
        fine[x, 16:24] = edge[8 * x:8 * x + 8]

    own, nxt = None, None
    half_rows = []
    for x in range(5):
        a, b = fine[x, 0:16], fine[x, 1:17]
        red[x, pl.ds(0, 16, stride=2)] = a
        red[x, pl.ds(1, 16, stride=2)] = 0.5 * (a + b)
        red[x, 32:40] = fine[x, 16:24]
    for x in range(9):
        value = red[x // 2] if x % 2 == 0 else 0.5 * (red[x // 2] + red[x // 2 + 1])
        node_sum[x, 0:40] = node_sum[x, 0:40] + value
    keep_next = [keep_hi, keep_right]
    for x in range(8):
        here = node_sum[x, 0:32]
        after = node_sum[x + 1, 0:32]
        if x == 7:
            after = after * keep_right
        shifted = roll(node_sum[x], -1, 0)[0:32]
        last = (row[0:32] == 31) & last_y
        shifted = jnp.where(last, 0.0, shifted)
        out[0, x] = acc[0, x, 0:32] + (after - here)
        out[1, x] = acc[1, x, 0:32] + (shifted - here)
        out[2, x] = acc[2, x, 0:32] + (jnp.where(lane_end[0:32], 0.0, roll(here, -1, 1)) - here)


def solution(mesh):
    nx, ny = mesh.shape["gx"], mesh.shape["gy"]
    f32 = jnp.float32
    dma = pltpu.SemaphoreType.DMA

    def shards(right_side, classes, table):
        return pl.pallas_call(
            functools.partial(kernel, nx, ny),
            out_shape=jax.ShapeDtypeStruct(right_side.shape, f32),
            in_specs=[pl.BlockSpec(memory_space=pl.ANY), pl.BlockSpec(memory_space=pl.ANY),
                      pl.BlockSpec(memory_space=pltpu.SMEM)],
            out_specs=pl.BlockSpec(memory_space=pltpu.VMEM),
            scratch_shapes=[
                pltpu.VMEM((3, 14, ROWS, 128), f32),
                pltpu.VMEM((8, 32, 128), jnp.int32),
                pltpu.VMEM((16, ROWS, 128), f32),
                pltpu.VMEM((3, 14, ROWS, 128), f32),
                pltpu.VMEM((3, 14, ROWS, 128), f32),
                pltpu.VMEM((3, 8, ROWS, 128), f32),
                pltpu.VMEM((8, 2, 8, 128), f32),
                pltpu.VMEM((9, 2, 8, 128), f32),
                pltpu.VMEM((15, 2, 8, 128), f32),
                pltpu.VMEM((16, 2, 8, 128), f32),
                pltpu.VMEM((18, ROWS, 128), f32),
                pltpu.VMEM((9, ROWS, 128), f32),
                pltpu.VMEM((5, 40, 128), f32),
                pltpu.VMEM((19, 8, 128), f32),
                pltpu.VMEM((19, 8, 128), f32),
                pltpu.VMEM((19, 8, 128), f32),
                pltpu.VMEM((23, 8, 128), f32),
                pltpu.VMEM((23, 8, 128), f32),
                pltpu.VMEM((23, 8, 128), f32),
                pltpu.VMEM((2, 19, 8, 128), f32),
                pltpu.VMEM((19, 8, 128), f32),
                pltpu.VMEM((19, 8, 128), f32),
                pltpu.VMEM((19, 8, 128), f32),
                pltpu.VMEM((19, 8, 128), f32),
                pltpu.VMEM((5, 24, 128), f32),
                dma((2,)), dma((10,)), dma((10,)), dma((2,)), dma((2,)), dma((8,)), dma((8,)),
                dma((14,)), dma((14,)), dma((14,)), dma((14,)),
            ],
            compiler_params=pltpu.CompilerParams(
                collective_id=0, has_side_effects=True, vmem_limit_bytes=40 * 2**20),
            name="cycle",
        )(right_side, classes, table)

    return jax.shard_map(
        shards,
        mesh=mesh,
        in_specs=(P(None, "gx", "gy", None), P("gx", "gy", None), P()),
        out_specs=P(None, "gx", "gy", None),
        check_vma=False,
    )
```

time: 390 us -> 55.1 us (0.14)
  the two profiles are of different devices: /device:TPU:35 before, /device:TPU:1 now
where the time goes in v1:
time: 55.1 us; the launch traced here: 54.8 us
  Pallas kernels  51.5 us (93%)
  local copies, waits for them, and re-layouts  3.3 us (6%)
    pallas_call x1, Pallas kernels, shards(): pl.pallas_call(functools.partial(kernel, nx, ny), out_shape=jax.ShapeDtyp...  51.5 us
    unnamed x7, local copies, waits for them, and re-layouts  3.3 us

profile of v1, /device:TPU:1, one launch (start us, length us, event | category | flops | bytes accessed | tf_op | source)
XLA Modules:
  0.0 54.8 jit_solution(14879783699149144839)
XLA Ops:
  0.0 0.0 copy-start
  0.0 1.0 %copy-done = f32[3,8,32,128]{3,2,1,0:T(8,128)S(1)} copy-done((f32[3,8,32,128]{3,2,1,0:T(8,128)S(1)}, f32[3,8,32,128]{3,2,1,0:T(8,128)}, u32[]{:S(2)}) %copy-start) | copy-done | bytes 393240
  1.0 0.0 copy-start.1
  1.0 0.9 %copy-done.1 = s32[8,32,128]{2,1,0:T(8,128)S(1)} copy-done((s32[8,32,128]{2,1,0:T(8,128)S(1)}, s32[8,32,128]{2,1,0:T(8,128)}, u32[]{:S(2)}) %copy-start.1) | copy-done | bytes 131096
  1.9 0.0 copy-start.2
  1.9 0.7 %copy-done.2 = f32[16]{0:T(128)S(1)} copy-done((f32[16]{0:T(128)S(1)}, f32[16]{0:T(128)}, u32[]{:S(2)}) %copy-start.2) | copy-done | bytes 88
  2.6 51.5 %cycle.1 = f32[3,8,32,128]{3,2,1,0:T(8,128)S(1)} custom-call(f32[3,8,32,128]{3,2,1,0:T(8,128)S(1)} %copy-done, s32[8,32,128]{2,1,0:T(8,128)S(1)} %copy-done.1, f32[16]{0:T(128)S(1)} %copy-done.2), custom_call_target="tpu_custom_call" | custom-call | tf_op jit(solution)/shard_map/cycle/pallas_call | solution.py:510
  54.0 0.7 %copy.5 = f32[3,8,32,128]{3,2,1,0:T(8,128)} copy(f32[3,8,32,128]{3,2,1,0:T(8,128)S(1)} %cycle.1) | data formatting | bytes 786432
Async XLA Ops:
  0.0 1.0 %copy-start = (f32[3,8,32,128]{3,2,1,0:T(8,128)S(1)}, f32[3,8,32,128]{3,2,1,0:T(8,128)}, u32[]{:S(2)}) copy-start(f32[3,8,32,128]{3,2,1,0:T(8,128)} %rhs.1) | copy-start | bytes 1179652
  1.0 0.9 %copy-start.1 = (s32[8,32,128]{2,1,0:T(8,128)S(1)}, s32[8,32,128]{2,1,0:T(8,128)}, u32[]{:S(2)}) copy-start(s32[8,32,128]{2,1,0:T(8,128)} %classes.1) | copy-start | bytes 393220
  1.9 0.7 %copy-start.2 = (f32[16]{0:T(128)S(1)}, f32[16]{0:T(128)}, u32[]{:S(2)}) copy-start(f32[16]{0:T(128)} %table.1) | copy-start | bytes 196

commit v2 on v1

--- a/solution.py
+++ b/solution.py
@@ -30,8 +30,8 @@
 
 
 def kernel(nx, ny, rhs, classes, table, out, base, kinds, sig, upd, res, acc,
-           pack_dn, pack_up, got_dn, got_up, nod, node_sum, red, cs_main, cs_dn, cs_up,
-           cf_main, cf_dn, cf_up, cm_one, g_one, g_two, s_one, s_two, fine,
+           pack_dn, pack_up, got_dn, got_up, nod, node_sum, red, cs_main, cs_pack, cs_got, cs_far,
+           cf_main, cf_pack, cf_got, cf_far, values_in, cm_one, g_one, g_two, s_one, s_two, fine,
            sem_in, send, recv, far_send, far_recv, x2_send, x2_recv, cs_send, cs_recv, x3_send, x3_recv):
     gx, gy = lax.axis_index("gx"), lax.axis_index("gy")
     first_x, last_x, first_y, last_y = gx == 0, gx == nx - 1, gy == 0, gy == ny - 1
@@ -50,13 +50,27 @@
     barrier = pltpu.get_barrier_semaphore()
     for where in near + distant:
         pl.semaphore_signal(barrier, inc=1, device_id=at(*where), device_id_type=MESH)
-    load_rhs = pltpu.make_async_copy(rhs, base.at[:, 3:11, 0:32], sem_in.at[0])
-    load_kinds = pltpu.make_async_copy(classes, kinds, sem_in.at[1])
-    load_rhs.start()
-    load_kinds.start()
-
-    load_kinds.wait()
-    values = [table[k] for k in range(16)]
+    loads = [
+        pltpu.make_async_copy(table, values_in, sem_in.at[2]),
+        pltpu.make_async_copy(classes, kinds, sem_in.at[1]),
+        pltpu.make_async_copy(rhs, base.at[:, 3:11, 0:32], sem_in.at[0]),
+    ]
+    for copy in loads:
+        copy.start()
+
+    pl.semaphore_wait(barrier, len(near + distant))
+    x1 = (send, recv)
+    first = [
+        remote(rhs.at[:, 5:8], base.at[:, 0:3, 0:32], x1, 0, (1, 0)),
+        remote(rhs.at[1:3, 0:3], base.at[1:3, 11:14, 0:32], x1, 1, (-1, 0)),
+        remote(rhs.at[0:1, 0:2], base.at[0:1, 11:13, 0:32], x1, 10, (-1, 0)),
+    ]
+    for copy in first:
+        copy.start()
+    for copy in loads:
+        copy.wait()
+
+    values = [values_in[k] for k in range(16)]
     for x in range(8):
         code = kinds[x]
         level = values
@@ -64,16 +78,6 @@
             flag = (code & (1 << bit)) != 0
             level = [jnp.where(flag, level[2 * i + 1], level[2 * i]) for i in range(len(level) // 2)]
         sig[x + 4, 0:32] = level[0]
-    load_rhs.wait()
-
-    pl.semaphore_wait(barrier, len(near + distant))
-    x1 = (send, recv)
-    first = [
-        remote(base.at[:, 8:11, 0:32], base.at[:, 0:3, 0:32], x1, 0, (1, 0)),
-        remote(base.at[:, 3:6, 0:32], base.at[:, 11:14, 0:32], x1, 1, (-1, 0)),
-    ]
-    for copy in first:
-        copy.start()
 
     sub = lax.broadcasted_iota(jnp.int32, (8, 128), 0)
     lower = sub < 4
@@ -157,8 +161,66 @@
     cm_one[0] = jnp.where(plane_ok, 1.0, 0.0)
     cm_one[1] = jnp.where(plane_ok, jnp.where(left3, keep_hi, keep_lo), 0.0)
 
+    left = lax.broadcasted_iota(jnp.int32, (8, 128), 1) < 64
+
+    def flip(tile):
+        return roll(tile, 64, 1)
+
+    def halves(a, b):
+        if b is None:
+            return a, flip(a)
+        return jnp.where(left, a, flip(b)), jnp.where(left, flip(a), b)
+
+    def unhalve(dn, up):
+        return jnp.where(left, dn, flip(up)), jnp.where(left, flip(dn), up)
+
+    def spread(main, pack, got, far_got, sems, own, count):
+        tiles = [main[own + i] for i in range(count)] + [None]
+        pairs = [halves(tiles[0], tiles[1]), halves(tiles[2], tiles[3])]
+        odd = [halves(tiles[1], tiles[2]), halves(tiles[3], tiles[4])]
+        if count == 5:
+            pairs.append(halves(tiles[4], None))
+        number = len(pairs)
+        for i, (dn, up) in enumerate(pairs):
+            pack[0, i] = dn
+            pack[1, i] = up
+        for i, (one, two) in enumerate((odd, pairs[:2])):
+            pack[0, 3 + i] = jnp.where(lower, one[0], roll(two[0], 4, 0))
+            pack[1, 3 + i] = jnp.where(lower, roll(one[1], 4, 0), two[1])
+        block = main.at[own:own + count]
+        size, end = count - 1, own + 2 * count
+        copies = [
+            remote(main.at[own + 1:own + count], main.at[0:size], sems, 0, (2, 0)),
+            remote(main.at[own:own + 4], main.at[end:end + 4], sems, 1, (-2, 0)),
+        ]
+        for i, dx in enumerate((2, -2)):
+            for j, dy in enumerate((-1, 1)):
+                copies.append(remote(pack.at[j, 3 + i], far_got.at[i, j], sems, 2 + 2 * i + j, (dx, dy)))
+        for i, dx in enumerate((1, -1, 0)):
+            for j, dy in enumerate((-1, 1)):
+                copies.append(remote(pack.at[j, 0:number], got.at[i, j, 0:number], sems, 6 + 2 * i + j, (dx, dy)))
+        copies.append(remote(block, main.at[own - count:own], sems, 12, (1, 0)))
+        copies.append(remote(block, main.at[own + count:own + 2 * count], sems, 13, (-1, 0)))
+        for copy in copies:
+            copy.start()
+        return copies
+
+    def received(got, far_got, number):
+        planes = []
+        for spot in (0, 2, 1):
+            block = []
+            for i in range(number):
+                block += list(unhalve(got[spot, 0, i], got[spot, 1, i]))
+            planes.append(block[:5] if number == 3 else block)
+        sides = []
+        for i in range(2):
+            dn, up = far_got[i, 0], far_got[i, 1]
+            sides.append(list(unhalve(dn, roll(up, 4, 0))) + list(unhalve(roll(dn, 4, 0), up)))
+        return sides[0], planes[0], planes[1], planes[2], sides[1]
+
     for copy in first + second:
         copy.wait()
+    cs_copies = spread(cs_main, cs_pack, cs_got, cs_far, (cs_send, cs_recv), 7, 4)
 
     def spot_dn(x):
         return x if 0 <= x < 8 else (12 + x if x < 0 else 4 + x)
@@ -225,7 +287,7 @@
                     (before[0] - cy) - (prev_y_inside(cx) - cx) + sg * uz,
                 ]
                 weight = scaled if side(x) is None else scaled * side(x)
-                left = []
+                rest = []
                 for c in range(3):
                     if turn == 0:
                         u = here[c] * inv
@@ -242,9 +304,9 @@
                     else:
                         answer = acc[c, x] + new
                         acc[c, x] = answer
-                        left.append(base[c, x + 3] - sg * answer)
+                        rest.append(base[c, x + 3] - sg * answer)
                 if turn == 2:
-                    rx, ry, rz = left
+                    rx, ry, rz = rest
                     total = (ry - prev_y(ry)) + (rz - prev_z(rz)) + rx
                     nod[x + 5, 0:32] = (total if nodal_prev is None else total - nodal_prev)[0:32]
                     nodal_prev = rx
@@ -265,34 +327,6 @@
         remote(nod.at[5:14, 0:8], nod.at[5:14, 32:40], x2, 7, (0, -1)),
     ]
     for copy in swap:
-        copy.start()
-
-    csem = (cs_send, cs_recv)
-
-    def spread(main, dn, up, sems, own, count):
-        block = main.at[own:own + count]
-        span = {1: own - count, -1: own + count}
-        copies = []
-        for k, dx in enumerate((1, -1)):
-            spot = span[dx]
-            copies.append(remote(block, main.at[spot:spot + count], sems, 6 * k, (dx, 0)))
-            copies.append(remote(block, dn.at[spot:spot + count], sems, 6 * k + 1, (dx, -1)))
-            copies.append(remote(block, up.at[spot:spot + count], sems, 6 * k + 2, (dx, 1)))
-        far_low, far_high = main.at[own + 1:own + count], main.at[own:own + 4]
-        size = count - 1
-        end = own + 2 * count
-        copies.append(remote(far_low, main.at[0:size], sems, 3, (2, 0)))
-        copies.append(remote(far_low, dn.at[0:size], sems, 4, (2, -1)))
-        copies.append(remote(far_low, up.at[0:size], sems, 5, (2, 1)))
-        copies.append(remote(far_high, main.at[end:end + 4], sems, 9, (-2, 0)))
-        copies.append(remote(far_high, dn.at[end:end + 4], sems, 10, (-2, -1)))
-        copies.append(remote(far_high, up.at[end:end + 4], sems, 11, (-2, 1)))
-        copies.append(remote(block, dn.at[own:own + count], sems, 12, (0, -1)))
-        copies.append(remote(block, up.at[own:own + count], sems, 13, (0, 1)))
-        return copies
-
-    cs_copies = spread(cs_main, cs_dn, cs_up, csem, 7, 4)
-    for copy in cs_copies:
         copy.start()
 
     for copy in later + swap:
@@ -377,32 +411,31 @@
     coarse = dot(wide, rest_z)
     for x in range(5):
         cf_main[9 + x] = coarse[8 * x:8 * x + 8]
-    cf_copies = spread(cf_main, cf_dn, cf_up, (x3_send, x3_recv), 9, 5)
-    for copy in cf_copies:
-        copy.start()
+    cf_copies = spread(cf_main, cf_pack, cf_got, cf_far, (x3_send, x3_recv), 9, 5)
     for copy in cs_copies:
         copy.wait()
 
-    left = lax.broadcasted_iota(jnp.int32, (8, 128), 1) < 64
+    far_low, low_block, own_block, high_block, far_high = received(cs_got, cs_far, 2)
+    halo = far_low[:3] + low_block + own_block + high_block + far_high
     for x in range(19):
         s_one[x] = cs_main[x] * cm_one[0, x]
-        s_two[x] = jnp.where(left, cs_dn[x], cs_up[x]) * cm_one[1, x]
+        s_two[x] = halo[x] * cm_one[1, x]
 
     for copy in cf_copies:
         copy.wait()
 
-    def joined(i):
-        return cf_main[i], jnp.where(left, cf_dn[i], cf_up[i])
-
+    far_low, low_block, own_block, high_block, far_high = received(cf_got, cf_far, 3)
+    halo = far_low + low_block + own_block + high_block + far_high
     where_plane = [0, 1, 2, 4, 5, 6, 7, 9, 10, 11, 12, 14, 15, 16, 17, 19, 20, 21, 22]
     extra = {-4: (3, gx > 1), 0: (8, gx > 0), 4: (13, None), 8: (18, None)}
     for x in range(-7, 12):
-        one, two = joined(where_plane[x + 7])
+        one, two = cf_main[where_plane[x + 7]], halo[where_plane[x + 7]]
         if x in extra:
             spot, valid = extra[x]
-            add_one, add_two = joined(spot)
-            scale = 1.0 if valid is None else f32(valid)
-            one, two = one + scale * add_one, two + scale * add_two
+            add_one, add_two = cf_main[spot], halo[spot]
+            if valid is not None:
+                add_one, add_two = add_one * f32(valid), add_two * f32(valid)
+            one, two = one + add_one, two + add_two
         g_one[x + 7] = one * cm_one[0, x + 7]
         g_two[x + 7] = two * cm_one[1, x + 7]
 
@@ -510,8 +543,7 @@
         return pl.pallas_call(
             functools.partial(kernel, nx, ny),
             out_shape=jax.ShapeDtypeStruct(right_side.shape, f32),
-            in_specs=[pl.BlockSpec(memory_space=pl.ANY), pl.BlockSpec(memory_space=pl.ANY),
-                      pl.BlockSpec(memory_space=pltpu.SMEM)],
+            in_specs=[pl.BlockSpec(memory_space=pltpu.HBM)] * 3,
             out_specs=pl.BlockSpec(memory_space=pltpu.VMEM),
             scratch_shapes=[
                 pltpu.VMEM((3, 14, ROWS, 128), f32),
@@ -528,24 +560,27 @@
                 pltpu.VMEM((9, ROWS, 128), f32),
                 pltpu.VMEM((5, 40, 128), f32),
                 pltpu.VMEM((19, 8, 128), f32),
-                pltpu.VMEM((19, 8, 128), f32),
-                pltpu.VMEM((19, 8, 128), f32),
+                pltpu.VMEM((2, 5, 8, 128), f32),
+                pltpu.VMEM((3, 2, 2, 8, 128), f32),
+                pltpu.VMEM((2, 2, 8, 128), f32),
                 pltpu.VMEM((23, 8, 128), f32),
-                pltpu.VMEM((23, 8, 128), f32),
-                pltpu.VMEM((23, 8, 128), f32),
+                pltpu.VMEM((2, 5, 8, 128), f32),
+                pltpu.VMEM((3, 2, 3, 8, 128), f32),
+                pltpu.VMEM((2, 2, 8, 128), f32),
+                pltpu.SMEM((16,), f32),
                 pltpu.VMEM((2, 19, 8, 128), f32),
                 pltpu.VMEM((19, 8, 128), f32),
                 pltpu.VMEM((19, 8, 128), f32),
                 pltpu.VMEM((19, 8, 128), f32),
                 pltpu.VMEM((19, 8, 128), f32),
                 pltpu.VMEM((5, 24, 128), f32),
-                dma((2,)), dma((10,)), dma((10,)), dma((2,)), dma((2,)), dma((8,)), dma((8,)),
+                dma((3,)), dma((11,)), dma((11,)), dma((2,)), dma((2,)), dma((8,)), dma((8,)),
                 dma((14,)), dma((14,)), dma((14,)), dma((14,)),
             ],
             compiler_params=pltpu.CompilerParams(
                 collective_id=0, has_side_effects=True, vmem_limit_bytes=40 * 2**20),
             name="cycle",
-        )(right_side, classes, table)
+        )(*(pltpu.with_memory_space_constraint(a, pltpu.HBM) for a in (right_side, classes, table)))
 
     return jax.shard_map(
         shards,

time: 55.1 us -> 48 us (0.87)
  Pallas kernels: 51.5 us -> 47.2 us
  local copies, waits for them, and re-layouts: 3.3 us -> 0.75 us
    pallas_call x1, Pallas kernels: 51.5 us -> 47.2 us  [shards(): pl.pallas_call(functools.partial(kernel, nx, ny), out_shape=jax.ShapeDtyp...]
    unnamed x7 -> x1, local copies, waits for them, and re-layouts: 3.3 us -> 0.75 us
where the time goes in v2:
time: 48 us
  Pallas kernels  47.2 us (98%)
  local copies, waits for them, and re-layouts  0.75 us (2%)
    pallas_call x1, Pallas kernels, shards(): pl.pallas_call(functools.partial(kernel, nx, ny), out_shape=jax.ShapeDtyp...  47.2 us

profile of v2, /device:TPU:1, one launch (start us, length us, event | category | flops | bytes accessed | tf_op | source)
XLA Modules:
  0.0 48.0 jit_solution(15163532557170641903)
XLA Ops:
  0.0 47.2 %cycle.1 = f32[3,8,32,128]{3,2,1,0:T(8,128)S(1)} custom-call(f32[3,8,32,128]{3,2,1,0:T(8,128)} %rhs.1, s32[8,32,128]{2,1,0:T(8,128)} %classes.1, f32[16]{0:T(128)} %table.1), custom_call_target="tpu_custom_call" | custom-call | tf_op jit(solution)/shard_map/cycle/pallas_call | solution.py:543
  47.2 0.7 %copy.5 = f32[3,8,32,128]{3,2,1,0:T(8,128)} copy(f32[3,8,32,128]{3,2,1,0:T(8,128)S(1)} %cycle.1) | data formatting | bytes 786432

commit v3 on v2

--- a/solution.py
+++ b/solution.py
@@ -39,8 +39,7 @@
     def at(dx, dy):
         return (lax.rem(gx + dx + nx, nx), lax.rem(gy + dy + ny, ny))
 
-    near = [(1, 0), (-1, 0), (0, 1), (0, -1), (1, 1), (1, -1), (-1, 1), (-1, -1)]
-    distant = [(2, 0), (-2, 0), (2, 1), (2, -1), (-2, 1), (-2, -1)]
+    near = [(1, 1), (1, -1), (-1, 1), (-1, -1), (1, 0), (-1, 0), (0, 1), (0, -1)]
 
     def remote(source, target, sems, index, where):
         return pltpu.make_async_remote_copy(
@@ -48,7 +47,7 @@
             device_id=at(*where), device_id_type=MESH)
 
     barrier = pltpu.get_barrier_semaphore()
-    for where in near + distant:
+    for where in near:
         pl.semaphore_signal(barrier, inc=1, device_id=at(*where), device_id_type=MESH)
     loads = [
         pltpu.make_async_copy(table, values_in, sem_in.at[2]),
@@ -58,7 +57,7 @@
     for copy in loads:
         copy.start()
 
-    pl.semaphore_wait(barrier, len(near + distant))
+    pl.semaphore_wait(barrier, len(near))
     x1 = (send, recv)
     first = [
         remote(rhs.at[:, 5:8], base.at[:, 0:3, 0:32], x1, 0, (1, 0)),
@@ -111,8 +110,6 @@
         remote(sig.at[8:10, 0:32], sig.at[0:2, 0:32], far, 0, (1, 0)),
         remote(sig.at[6:7, 0:32], sig.at[14:15, 0:32], far, 1, (-1, 0)),
     ]
-    for copy in later:
-        copy.start()
 
     lane = lax.broadcasted_iota(jnp.int32, (ROWS, 128), 1)
     row = lax.broadcasted_iota(jnp.int32, (ROWS, 128), 0)
@@ -189,21 +186,20 @@
             pack[1, 3 + i] = jnp.where(lower, roll(one[1], 4, 0), two[1])
         block = main.at[own:own + count]
         size, end = count - 1, own + 2 * count
-        copies = [
+        distant = [
             remote(main.at[own + 1:own + count], main.at[0:size], sems, 0, (2, 0)),
             remote(main.at[own:own + 4], main.at[end:end + 4], sems, 1, (-2, 0)),
         ]
         for i, dx in enumerate((2, -2)):
             for j, dy in enumerate((-1, 1)):
-                copies.append(remote(pack.at[j, 3 + i], far_got.at[i, j], sems, 2 + 2 * i + j, (dx, dy)))
+                distant.append(remote(pack.at[j, 3 + i], far_got.at[i, j], sems, 2 + 2 * i + j, (dx, dy)))
+        close = []
         for i, dx in enumerate((1, -1, 0)):
             for j, dy in enumerate((-1, 1)):
-                copies.append(remote(pack.at[j, 0:number], got.at[i, j, 0:number], sems, 6 + 2 * i + j, (dx, dy)))
-        copies.append(remote(block, main.at[own - count:own], sems, 12, (1, 0)))
-        copies.append(remote(block, main.at[own + count:own + 2 * count], sems, 13, (-1, 0)))
-        for copy in copies:
-            copy.start()
-        return copies
+                close.append(remote(pack.at[j, 0:number], got.at[i, j, 0:number], sems, 6 + 2 * i + j, (dx, dy)))
+        close.append(remote(block, main.at[own - count:own], sems, 12, (1, 0)))
+        close.append(remote(block, main.at[own + count:own + 2 * count], sems, 13, (-1, 0)))
+        return distant, close
 
     def received(got, far_got, number):
         planes = []
@@ -220,7 +216,9 @@
 
     for copy in first + second:
         copy.wait()
-    cs_copies = spread(cs_main, cs_pack, cs_got, cs_far, (cs_send, cs_recv), 7, 4)
+    cs_distant, cs_close = spread(cs_main, cs_pack, cs_got, cs_far, (cs_send, cs_recv), 7, 4)
+    for copy in later + cs_close:
+        copy.start()
 
     def spot_dn(x):
         return x if 0 <= x < 8 else (12 + x if x < 0 else 4 + x)
@@ -326,7 +324,7 @@
         remote(nod.at[5:14, 24:32], nod.at[5:14, 40:48], x2, 6, (0, 1)),
         remote(nod.at[5:14, 0:8], nod.at[5:14, 32:40], x2, 7, (0, -1)),
     ]
-    for copy in swap:
+    for copy in swap + cs_distant:
         copy.start()
 
     for copy in later + swap:
@@ -411,8 +409,10 @@
     coarse = dot(wide, rest_z)
     for x in range(5):
         cf_main[9 + x] = coarse[8 * x:8 * x + 8]
-    cf_copies = spread(cf_main, cf_pack, cf_got, cf_far, (x3_send, x3_recv), 9, 5)
-    for copy in cs_copies:
+    cf_distant, cf_close = spread(cf_main, cf_pack, cf_got, cf_far, (x3_send, x3_recv), 9, 5)
+    for copy in cf_distant + cf_close:
+        copy.start()
+    for copy in cs_distant + cs_close:
         copy.wait()
 
     far_low, low_block, own_block, high_block, far_high = received(cs_got, cs_far, 2)
@@ -421,7 +421,7 @@
         s_one[x] = cs_main[x] * cm_one[0, x]
         s_two[x] = halo[x] * cm_one[1, x]
 
-    for copy in cf_copies:
+    for copy in cf_distant + cf_close:
         copy.wait()
 
     far_low, low_block, own_block, high_block, far_high = received(cf_got, cf_far, 3)

time: 48 us -> 46.4 us (0.967)
  Pallas kernels: 47.2 us -> 45.6 us
    pallas_call x1, Pallas kernels: 47.2 us -> 45.6 us  [shards(): pl.pallas_call(functools.partial(kernel, nx, ny), out_shape=jax.ShapeDtyp...]
where the time goes in v3:
time: 46.4 us
  Pallas kernels  45.6 us (98%)
  local copies, waits for them, and re-layouts  0.75 us (2%)
    pallas_call x1, Pallas kernels, shards(): pl.pallas_call(functools.partial(kernel, nx, ny), out_shape=jax.ShapeDtyp...  45.6 us

profile of v3, /device:TPU:1, one launch (start us, length us, event | category | flops | bytes accessed | tf_op | source)
XLA Modules:
  0.0 46.4 jit_solution(10380641113061357752)
XLA Ops:
  0.0 45.6 %cycle.1 = f32[3,8,32,128]{3,2,1,0:T(8,128)S(1)} custom-call(f32[3,8,32,128]{3,2,1,0:T(8,128)} %rhs.1, s32[8,32,128]{2,1,0:T(8,128)} %classes.1, f32[16]{0:T(128)} %table.1), custom_call_target="tpu_custom_call" | custom-call | tf_op jit(solution)/shard_map/cycle/pallas_call | solution.py:543
  45.6 0.7 %copy.5 = f32[3,8,32,128]{3,2,1,0:T(8,128)} copy(f32[3,8,32,128]{3,2,1,0:T(8,128)S(1)} %cycle.1) | data formatting | bytes 786432

commit v4 on v3

--- a/solution.py
+++ b/solution.py
@@ -29,9 +29,9 @@
     return pltpu.roll(value, shift % value.shape[axis], axis)
 
 
-def kernel(nx, ny, rhs, classes, table, out, base, kinds, sig, upd, res, acc,
+def kernel(nx, ny, rhs, classes, table, out, base, kinds, sig, upd, upd_next, drop, res, acc,
            pack_dn, pack_up, got_dn, got_up, nod, node_sum, red, cs_main, cs_pack, cs_got, cs_far,
-           cf_main, cf_pack, cf_got, cf_far, values_in, cm_one, g_one, g_two, s_one, s_two, fine,
+           cf_main, cf_pack, cf_got, cf_far, values_in, cm_one, g_one, g_two, s_one, s_two, s_back, fine,
            sem_in, send, recv, far_send, far_recv, x2_send, x2_recv, cs_send, cs_recv, x3_send, x3_recv):
     gx, gy = lax.axis_index("gx"), lax.axis_index("gy")
     first_x, last_x, first_y, last_y = gx == 0, gx == nx - 1, gy == 0, gy == ny - 1
@@ -60,9 +60,10 @@
     pl.semaphore_wait(barrier, len(near))
     x1 = (send, recv)
     first = [
-        remote(rhs.at[:, 5:8], base.at[:, 0:3, 0:32], x1, 0, (1, 0)),
         remote(rhs.at[1:3, 0:3], base.at[1:3, 11:14, 0:32], x1, 1, (-1, 0)),
+        remote(rhs.at[1:3, 5:8], base.at[1:3, 0:3, 0:32], x1, 0, (1, 0)),
         remote(rhs.at[0:1, 0:2], base.at[0:1, 11:13, 0:32], x1, 10, (-1, 0)),
+        remote(rhs.at[0:1, 5:8], base.at[0:1, 0:3, 0:32], x1, 11, (1, 0)),
     ]
     for copy in first:
         copy.start()
@@ -103,7 +104,7 @@
         remote(sig.at[10:12, 0:32], sig.at[2:4, 0:32], x1, 8, (1, 0)),
         remote(sig.at[4:6, 0:32], sig.at[12:14, 0:32], x1, 9, (-1, 0)),
     ]
-    for copy in second:
+    for copy in second[4:6] + second[0:4] + second[6:8]:
         copy.start()
     far = (far_send, far_recv)
     later = [
@@ -141,7 +142,16 @@
     apart = (fine_z % 128) - 2 * (packed_z % 64)
     mean_z = jnp.where(half & ((apart == 0) | (apart == 1)), 0.125, 0.0)
     rest_z = jnp.where(half, jnp.where(apart == 0, 1.0, jnp.where(jnp.abs(apart) == 1, 0.5, 0.0)), 0.0)
-    dot = functools.partial(jnp.dot, precision=lax.Precision.HIGHEST, preferred_element_type=jnp.float32)
+
+    def dot(value, weights):
+        weights = weights.astype(jnp.bfloat16)
+        total = None
+        for _ in range(3):
+            part = value.astype(jnp.bfloat16)
+            value = value - part.astype(jnp.float32)
+            product = jnp.dot(part, weights, preferred_element_type=jnp.float32)
+            total = product if total is None else total + product
+        return total
 
     for x in range(4):
         red[x, 8:40] = sig[2 * x + 4, 0:32] + sig[2 * x + 5, 0:32]
@@ -214,11 +224,7 @@
             sides.append(list(unhalve(dn, roll(up, 4, 0))) + list(unhalve(roll(dn, 4, 0), up)))
         return sides[0], planes[0], planes[1], planes[2], sides[1]
 
-    for copy in first + second:
-        copy.wait()
     cs_distant, cs_close = spread(cs_main, cs_pack, cs_got, cs_far, (cs_send, cs_recv), 7, 4)
-    for copy in later + cs_close:
-        copy.start()
 
     def spot_dn(x):
         return x if 0 <= x < 8 else (12 + x if x < 0 else 4 + x)
@@ -227,50 +233,43 @@
         return x if 0 <= x < 8 else (13 + x if x < 0 else 5 + x)
 
     zero_tile = jnp.zeros((8, 128), jnp.float32)
-    for x in range(-4, 11):
-        if x > -4:
-            a, b = got_dn[spot_dn(x), 0], got_dn[spot_dn(x), 1]
-            base[0, x + 3, 32:40] = a * keep_hi
-            base[1, x + 3, 32:40] = roll(a, 4, 0) * keep_hi
-            base[2, x + 3, 32:40] = b * keep_hi
-            sig[x + 4, 32:40] = roll(b, 4, 0) * keep_hi
-        else:
-            sig[x + 4, 32:40] = zero_tile
-        a, b = got_up[spot_up(x), 0], got_up[spot_up(x), 1]
-        if x > -4:
-            base[0, x + 3, 40:48] = a * keep_lo
-            base[1, x + 3, 40:48] = roll(a, 4, 0) * keep_lo
-            base[2, x + 3, 40:48] = b * keep_lo
-        sg = roll(b, 4, 0)
-        if 0 <= x < 8:
-            sg = jnp.where(sub == 3, got_up[8, 0, x:x + 1], sg)
-        sig[x + 4, 40:48] = sg * keep_lo
-
-    @pl.when(first_x)
-    def _():
-        base[:, 0:3] = jnp.zeros((3, 3, ROWS, 128), jnp.float32)
-        sig[2:4] = jnp.zeros((2, ROWS, 128), jnp.float32)
-
-    @pl.when(last_x)
-    def _():
-        base[:, 11:14] = jnp.zeros((3, 3, ROWS, 128), jnp.float32)
-        sig[12:14] = jnp.zeros((2, ROWS, 128), jnp.float32)
+
+    def unpack(planes):
+        for x in planes:
+            if x > -4:
+                a, b = got_dn[spot_dn(x), 0], got_dn[spot_dn(x), 1]
+                base[0, x + 3, 32:40] = a * keep_hi
+                base[1, x + 3, 32:40] = roll(a, 4, 0) * keep_hi
+                base[2, x + 3, 32:40] = b * keep_hi
+                sig[x + 4, 32:40] = roll(b, 4, 0) * keep_hi
+            else:
+                sig[x + 4, 32:40] = zero_tile
+            a, b = got_up[spot_up(x), 0], got_up[spot_up(x), 1]
+            if x > -4:
+                base[0, x + 3, 40:48] = a * keep_lo
+                base[1, x + 3, 40:48] = roll(a, 4, 0) * keep_lo
+                base[2, x + 3, 40:48] = b * keep_lo
+            sg = roll(b, 4, 0)
+            if 0 <= x < 8:
+                sg = jnp.where(sub == 3, got_up[8, 0, x:x + 1], sg)
+            sig[x + 4, 40:48] = sg * keep_lo
 
     keep_left, keep_right = 1.0 - f32(first_x), 1.0 - f32(last_x)
 
     def side(x):
         return keep_left if x < 0 else (keep_right if x > 7 else None)
 
-    inv, steps = coefficients(20.0, 30.0, 4)
-    nodal_prev = None
-    for turn, (c_old, c_res) in enumerate(steps):
-        lo, hi = -2 + turn, 9 - turn
-        get = (lambda c, x: base[c, x + 3]) if turn == 0 else (lambda c, x: upd[c, x + 2])
+    inv, edge_steps = coefficients(20.0, 30.0, 4)
+
+    def edge_turn(turn, lo, hi):
+        c_old, c_res = edge_steps[turn]
+        source, target = ((base, upd), (upd, upd_next), (upd_next, None))[turn]
+        shift = 3 if turn == 0 else 2
         scaled = row_mask * c_res
         before = None
-        here = [get(c, lo - 1) for c in range(3)]
+        here = [source[c, lo - 1 + shift] for c in range(3)]
         for x in range(lo - 1, hi + 1):
-            after = [None if (c == 0 and x == hi) else get(c, x + 1) for c in range(3)]
+            after = [None if (c == 0 and x == hi) else source[c, x + 1 + shift] for c in range(3)]
             ux, uy, uz = here
             cy = (next_z(ux) - ux) - (after[2] - uz)
             cz = (after[1] - uy) - (next_y(ux) - ux)
@@ -295,7 +294,7 @@
                         r = res[c, x + 2] - applied[c]
                     new = c_old * u + weight * r
                     if turn < 2:
-                        upd[c, x + 2] = new
+                        target[c, x + 2] = new
                         res[c, x + 2] = r
                         if 0 <= x < 8:
                             acc[c, x] = u + new if turn == 0 else acc[c, x] + new
@@ -306,12 +305,33 @@
                 if turn == 2:
                     rx, ry, rz = rest
                     total = (ry - prev_y(ry)) + (rz - prev_z(rz)) + rx
-                    nod[x + 5, 0:32] = (total if nodal_prev is None else total - nodal_prev)[0:32]
-                    nodal_prev = rx
-                    if x == 7:
-                        nod[13, 0:32] = rx[0:32]
+                    if x not in (0, lo) or x == 5:
+                        total = total - drop[x - 1]
+                    nod[x + 5, 0:32] = total[0:32]
+                    drop[x] = rx
             before = (cy, cz)
             here = after
+
+    for copy in (second[4], second[5]):
+        copy.wait()
+    unpack(range(8))
+    edge_turn(0, 1, 6)
+    edge_turn(1, 2, 5)
+    edge_turn(2, 3, 4)
+
+    for copy in (first[0], first[2], second[0], second[1], second[7]):
+        copy.wait()
+    unpack(range(8, 11))
+
+    @pl.when(last_x)
+    def _():
+        base[:, 11:14] = jnp.zeros((3, 3, ROWS, 128), jnp.float32)
+        sig[12:14] = jnp.zeros((2, ROWS, 128), jnp.float32)
+
+    edge_turn(0, 7, 9)
+    edge_turn(1, 6, 8)
+    edge_turn(2, 5, 7)
+    nod[13, 0:32] = drop[7, 0:32]
 
     x2 = (x2_send, x2_recv)
     swap = [
@@ -324,7 +344,27 @@
         remote(nod.at[5:14, 24:32], nod.at[5:14, 40:48], x2, 6, (0, 1)),
         remote(nod.at[5:14, 0:8], nod.at[5:14, 32:40], x2, 7, (0, -1)),
     ]
-    for copy in swap + cs_distant:
+    for copy in (swap[2], swap[3], swap[0]):
+        copy.start()
+
+    for copy in (first[1], first[3], second[2], second[3], second[6]):
+        copy.wait()
+    for copy in later + cs_close:
+        copy.start()
+    unpack(range(-4, 0))
+
+    @pl.when(first_x)
+    def _():
+        base[:, 0:3] = jnp.zeros((3, 3, ROWS, 128), jnp.float32)
+        sig[2:4] = jnp.zeros((2, ROWS, 128), jnp.float32)
+
+    edge_turn(0, -2, 0)
+    edge_turn(1, -1, 1)
+    edge_turn(2, 0, 2)
+    nod[8, 0:32] = nod[8, 0:32] - drop[2, 0:32]
+    for copy in (swap[4], swap[5], swap[1], swap[6], swap[7]):
+        copy.start()
+    for copy in cs_distant:
         copy.start()
 
     for copy in later + swap:
@@ -421,6 +461,29 @@
         s_one[x] = cs_main[x] * cm_one[0, x]
         s_two[x] = halo[x] * cm_one[1, x]
 
+    def lanes3(n):
+        return lax.broadcasted_iota(jnp.int32, (n, 8, 128), 2)
+
+    def coarse_both_y(one, two, ahead=True):
+        turn_one, turn_two = roll(one, 64, 2), roll(two, 64, 2)
+        pick = lanes3(one.shape[0]) < 64
+        mixed, other = jnp.where(pick, turn_one, turn_two), jnp.where(pick, turn_two, turn_one)
+        rows = lax.broadcasted_iota(jnp.int32, one.shape, 1)
+        behind = (roll(jnp.where(rows == 7, other, one), 1, 1), roll(jnp.where(rows == 7, mixed, two), 1, 1))
+        if not ahead:
+            return None, behind
+        return (roll(jnp.where(rows == 0, mixed, one), -1, 1), roll(jnp.where(rows == 0, other, two), -1, 1)), behind
+
+    def coarse_next_z(f):
+        return jnp.where(lanes3(f.shape[0]) % 64 == 63, 0.0, roll(f, -1, 2))
+
+    def coarse_prev_z(f):
+        return jnp.where(lanes3(f.shape[0]) % 64 == 0, 0.0, roll(f, 1, 2))
+
+    _, (back_one, back_two) = coarse_both_y(s_one[...], s_two[...], False)
+    s_back[0, 0], s_back[0, 1] = back_one, back_two
+    s_back[1, 0], s_back[1, 1] = coarse_prev_z(s_one[...]), coarse_prev_z(s_two[...])
+
     for copy in cf_distant + cf_close:
         copy.wait()
 
@@ -440,33 +503,6 @@
         g_two[x + 7] = two * cm_one[1, x + 7]
 
     inv, steps = coefficients(96.0, 100.0, 8)
-
-    def lanes3(n):
-        return lax.broadcasted_iota(jnp.int32, (n, 8, 128), 2)
-
-    def swapped(one, two, first_side):
-        turn_one, turn_two = roll(one, 64, 2), roll(two, 64, 2)
-        pick = lanes3(one.shape[0]) < 64
-        if first_side:
-            return jnp.where(pick, turn_one, turn_two), jnp.where(pick, turn_two, turn_one)
-        return jnp.where(pick, turn_two, turn_one), jnp.where(pick, turn_one, turn_two)
-
-    def coarse_next_y(one, two):
-        seam_one, seam_two = swapped(one, two, True)
-        top = lax.broadcasted_iota(jnp.int32, one.shape, 1) == 0
-        return roll(jnp.where(top, seam_one, one), -1, 1), roll(jnp.where(top, seam_two, two), -1, 1)
-
-    def coarse_prev_y(one, two):
-        seam_one, seam_two = swapped(one, two, False)
-        bottom = lax.broadcasted_iota(jnp.int32, one.shape, 1) == 7
-        return roll(jnp.where(bottom, seam_one, one), 1, 1), roll(jnp.where(bottom, seam_two, two), 1, 1)
-
-    def coarse_next_z(f):
-        return jnp.where(lanes3(f.shape[0]) % 64 == 63, 0.0, roll(f, -1, 2))
-
-    def coarse_prev_z(f):
-        return jnp.where(lanes3(f.shape[0]) % 64 == 0, 0.0, roll(f, 1, 2))
-
     f_one, f_two = g_one[...], g_two[...]
     r_one = r_two = None
     answer = None
@@ -477,15 +513,13 @@
         x_one = sg_one[:-1] * (f_one[1:] - f_one[:-1])
         x_two = sg_two[:-1] * (f_two[1:] - f_two[:-1])
         mid_one, mid_two = f_one[1:-1], f_two[1:-1]
-        in_one, in_two = sg_one[1:-1], sg_two[1:-1]
-        up_one, up_two = coarse_next_y(mid_one, mid_two)
-        y_one, y_two = in_one * (up_one - mid_one), in_two * (up_two - mid_two)
-        back_one, back_two = coarse_prev_y(y_one, y_two)
+        inner = slice(low + 8, low + 6 + n)
+        ahead_y, behind_y = coarse_both_y(mid_one, mid_two)
         results = []
-        for f, x_flux, y_flux, y_back, s in (
-            (mid_one, x_one, y_one, back_one, in_one), (mid_two, x_two, y_two, back_two, in_two)):
-            z_flux = s * (coarse_next_z(f) - f)
-            results.append((x_flux[1:] - x_flux[:-1]) + (y_flux - y_back) + (z_flux - coarse_prev_z(z_flux)))
+        for k, (f, x_flux, s) in enumerate(((mid_one, x_one, sg_one[1:-1]), (mid_two, x_two, sg_two[1:-1]))):
+            ahead = s * ((ahead_y[k] - f) + (coarse_next_z(f) - f))
+            behind = s_back[0, k, inner] * (behind_y[k] - f) + s_back[1, k, inner] * (roll(f, 1, 2) - f)
+            results.append((x_flux[1:] - x_flux[:-1]) + (ahead + behind))
         low += 1
         if turn == 0:
             r_one, r_two = mid_one - results[0] * inv, mid_two - results[1] * inv
@@ -550,6 +584,8 @@
                 pltpu.VMEM((8, 32, 128), jnp.int32),
                 pltpu.VMEM((16, ROWS, 128), f32),
                 pltpu.VMEM((3, 14, ROWS, 128), f32),
+                pltpu.VMEM((3, 14, ROWS, 128), f32),
+                pltpu.VMEM((8, ROWS, 128), f32),
                 pltpu.VMEM((3, 14, ROWS, 128), f32),
                 pltpu.VMEM((3, 8, ROWS, 128), f32),
                 pltpu.VMEM((8, 2, 8, 128), f32),
@@ -573,8 +609,9 @@
                 pltpu.VMEM((19, 8, 128), f32),
                 pltpu.VMEM((19, 8, 128), f32),
                 pltpu.VMEM((19, 8, 128), f32),
+                pltpu.VMEM((2, 2, 19, 8, 128), f32),
                 pltpu.VMEM((5, 24, 128), f32),
-                dma((3,)), dma((11,)), dma((11,)), dma((2,)), dma((2,)), dma((8,)), dma((8,)),
+                dma((3,)), dma((12,)), dma((12,)), dma((2,)), dma((2,)), dma((8,)), dma((8,)),
                 dma((14,)), dma((14,)), dma((14,)), dma((14,)),
             ],
             compiler_params=pltpu.CompilerParams(

time: 46.4 us -> 45.1 us (0.972)
  Pallas kernels: 45.6 us -> 44.3 us
    pallas_call x1, Pallas kernels: 45.6 us -> 44.3 us  [shards(): pl.pallas_call(functools.partial(kernel, nx, ny), out_shape=jax.ShapeDtyp...]
where the time goes in v4:
time: 45.1 us; the launch traced here: 45 us
  Pallas kernels  44.3 us (98%)
  local copies, waits for them, and re-layouts  0.75 us (2%)
    pallas_call x1, Pallas kernels, shards(): pl.pallas_call(functools.partial(kernel, nx, ny), out_shape=jax.ShapeDtyp...  44.3 us

profile of v4, /device:TPU:1, one launch (start us, length us, event | category | flops | bytes accessed | tf_op | source)
XLA Modules:
  0.0 45.0 jit_solution(2443182034149244931)
XLA Ops:
  0.0 44.3 %cycle.1 = f32[3,8,32,128]{3,2,1,0:T(8,128)S(1)} custom-call(f32[3,8,32,128]{3,2,1,0:T(8,128)} %rhs.1, s32[8,32,128]{2,1,0:T(8,128)} %classes.1, f32[16]{0:T(128)} %table.1), custom_call_target="tpu_custom_call" | custom-call | tf_op jit(solution)/shard_map/cycle/pallas_call | solution.py:577
  44.3 0.7 %copy.5 = f32[3,8,32,128]{3,2,1,0:T(8,128)} copy(f32[3,8,32,128]{3,2,1,0:T(8,128)S(1)} %cycle.1) | data formatting | bytes 786432

commit v5 on v4

--- a/solution.py
+++ b/solution.py
@@ -30,7 +30,7 @@
 
 
 def kernel(nx, ny, rhs, classes, table, out, base, kinds, sig, upd, upd_next, drop, res, acc,
-           pack_dn, pack_up, got_dn, got_up, nod, node_sum, red, cs_main, cs_pack, cs_got, cs_far,
+           pack_dn, pack_up, got_dn, got_up, turn_pack, turn_got, nod, node_sum, red, cs_main, cs_pack, cs_got, cs_far,
            cf_main, cf_pack, cf_got, cf_far, values_in, cm_one, g_one, g_two, s_one, s_two, s_back, fine,
            sem_in, send, recv, far_send, far_recv, x2_send, x2_recv, cs_send, cs_recv, x3_send, x3_recv):
     gx, gy = lax.axis_index("gx"), lax.axis_index("gy")
@@ -95,7 +95,7 @@
     pack_up[8, 1] = jnp.zeros((8, 128), jnp.float32)
 
     second = [
-        remote(pack_dn.at[0:3], got_dn.at[12:15], x1, 2, (-1, -1)),
+        remote(pack_dn.at[0:2], got_dn.at[12:14], x1, 2, (-1, -1)),
         remote(pack_up.at[0:3], got_up.at[13:16], x1, 3, (-1, 1)),
         remote(pack_dn.at[5:8], got_dn.at[9:12], x1, 4, (1, -1)),
         remote(pack_up.at[4:8], got_up.at[9:13], x1, 5, (1, 1)),
@@ -196,9 +196,10 @@
             pack[1, 3 + i] = jnp.where(lower, roll(one[1], 4, 0), two[1])
         block = main.at[own:own + count]
         size, end = count - 1, own + 2 * count
+        reach = 4 if count == 5 else 3
         distant = [
             remote(main.at[own + 1:own + count], main.at[0:size], sems, 0, (2, 0)),
-            remote(main.at[own:own + 4], main.at[end:end + 4], sems, 1, (-2, 0)),
+            remote(main.at[own:own + reach], main.at[end:end + reach], sems, 1, (-2, 0)),
         ]
         for i, dx in enumerate((2, -2)):
             for j, dy in enumerate((-1, 1)):
@@ -236,7 +237,11 @@
 
     def unpack(planes):
         for x in planes:
-            if x > -4:
+            if x == 10:
+                for c in range(3):
+                    base[c, x + 3, 32:40] = zero_tile
+                sig[x + 4, 32:40] = zero_tile
+            elif x > -4:
                 a, b = got_dn[spot_dn(x), 0], got_dn[spot_dn(x), 1]
                 base[0, x + 3, 32:40] = a * keep_hi
                 base[1, x + 3, 32:40] = roll(a, 4, 0) * keep_hi
@@ -337,13 +342,19 @@
     swap = [
         remote(nod.at[9:14, 0:32], nod.at[0:5, 0:32], x2, 0, (1, 0)),
         remote(nod.at[5:9, 0:32], nod.at[14:18, 0:32], x2, 1, (-1, 0)),
-        remote(nod.at[9:14, 24:32], nod.at[0:5, 40:48], x2, 2, (1, 1)),
-        remote(nod.at[9:14, 0:8], nod.at[0:5, 32:40], x2, 3, (1, -1)),
-        remote(nod.at[5:9, 24:32], nod.at[14:18, 40:48], x2, 4, (-1, 1)),
-        remote(nod.at[5:9, 0:8], nod.at[14:18, 32:40], x2, 5, (-1, -1)),
+        remote(turn_pack.at[0:2], turn_got.at[0:2], x2, 2, (1, 1)),
+        remote(turn_pack.at[2:4], turn_got.at[2:4], x2, 3, (1, -1)),
+        remote(turn_pack.at[4:6], turn_got.at[4:6], x2, 4, (-1, 1)),
+        remote(turn_pack.at[6], turn_got.at[6], x2, 5, (-1, -1)),
         remote(nod.at[5:14, 24:32], nod.at[5:14, 40:48], x2, 6, (0, 1)),
         remote(nod.at[5:14, 0:8], nod.at[5:14, 32:40], x2, 7, (0, -1)),
     ]
+    up = [nod[9 + i, 24:32] for i in range(5)]
+    turn_pack[0] = jnp.where(sub >= 3, up[4], jnp.where(sub == 0, roll(up[0], 1, 0), roll(up[1], 3, 0)))
+    turn_pack[1] = jnp.where(lower, roll(up[2], 4, 0), up[3])
+    dn = [nod[9 + i, 0:8] for i in range(5)]
+    turn_pack[2] = jnp.where(lower, dn[4], roll(dn[3], 4, 0))
+    turn_pack[3] = jnp.where(lower, dn[2], roll(dn[1], 4, 0))
     for copy in (swap[2], swap[3], swap[0]):
         copy.start()
 
@@ -362,6 +373,11 @@
     edge_turn(1, -1, 1)
     edge_turn(2, 0, 2)
     nod[8, 0:32] = nod[8, 0:32] - drop[2, 0:32]
+    up = [nod[5 + i, 24:32] for i in range(4)]
+    turn_pack[4] = jnp.where(lower, roll(up[1], 4, 0), up[0])
+    turn_pack[5] = jnp.where(lower, roll(up[3], 4, 0), up[2])
+    dn = [nod[5 + i, 0:8] for i in range(3)]
+    turn_pack[6] = jnp.where(lower, dn[0], jnp.where(sub < 6, roll(dn[1], 4, 0), roll(dn[2], 6, 0)))
     for copy in (swap[4], swap[5], swap[1], swap[6], swap[7]):
         copy.start()
     for copy in cs_distant:
@@ -369,6 +385,18 @@
 
     for copy in later + swap:
         copy.wait()
+    one, two = turn_got[0], turn_got[1]
+    for spot, tile in enumerate((roll(one, 7, 0), roll(one, 5, 0), roll(two, 4, 0), two, one)):
+        nod[spot, 40:48] = tile
+    one, two = turn_got[2], turn_got[3]
+    for spot, tile in enumerate((zero_tile, roll(two, 4, 0), two, roll(one, 4, 0), one)):
+        nod[spot, 32:40] = tile
+    one, two = turn_got[4], turn_got[5]
+    for spot, tile in enumerate((one, roll(one, 4, 0), two, roll(two, 4, 0))):
+        nod[14 + spot, 40:48] = tile
+    one = turn_got[6]
+    for spot, tile in enumerate((one, roll(one, 4, 0), roll(one, 2, 0), zero_tile)):
+        nod[14 + spot, 32:40] = tile
 
     @pl.when(first_x)
     def _():
@@ -457,9 +485,10 @@
 
     far_low, low_block, own_block, high_block, far_high = received(cs_got, cs_far, 2)
     halo = far_low[:3] + low_block + own_block + high_block + far_high
-    for x in range(19):
+    for x in range(18):
         s_one[x] = cs_main[x] * cm_one[0, x]
         s_two[x] = halo[x] * cm_one[1, x]
+    s_one[18], s_two[18] = zero_tile, zero_tile
 
     def lanes3(n):
         return lax.broadcasted_iota(jnp.int32, (n, 8, 128), 2)
@@ -592,6 +621,8 @@
                 pltpu.VMEM((9, 2, 8, 128), f32),
                 pltpu.VMEM((15, 2, 8, 128), f32),
                 pltpu.VMEM((16, 2, 8, 128), f32),
+                pltpu.VMEM((7, 8, 128), f32),
+                pltpu.VMEM((7, 8, 128), f32),
                 pltpu.VMEM((18, ROWS, 128), f32),
                 pltpu.VMEM((9, ROWS, 128), f32),
                 pltpu.VMEM((5, 40, 128), f32),

time: 45.1 us -> 44.2 us (0.980)
  Pallas kernels: 44.3 us -> 43.3 us
    pallas_call x1, Pallas kernels: 44.3 us -> 43.3 us  [shards(): pl.pallas_call(functools.partial(kernel, nx, ny), out_shape=jax.ShapeDtyp...]
where the time goes in v5:
time: 44.2 us; the launch traced here: 44.1 us
  Pallas kernels  43.3 us (98%)
  local copies, waits for them, and re-layouts  0.75 us (2%)
    pallas_call x1, Pallas kernels, shards(): pl.pallas_call(functools.partial(kernel, nx, ny), out_shape=jax.ShapeDtyp...  43.3 us

profile of v5, /device:TPU:1, one launch (start us, length us, event | category | flops | bytes accessed | tf_op | source)
XLA Modules:
  0.0 44.1 jit_solution(16602687965599843337)
XLA Ops:
  0.0 43.3 %cycle.1 = f32[3,8,32,128]{3,2,1,0:T(8,128)S(1)} custom-call(f32[3,8,32,128]{3,2,1,0:T(8,128)} %rhs.1, s32[8,32,128]{2,1,0:T(8,128)} %classes.1, f32[16]{0:T(128)} %table.1), custom_call_target="tpu_custom_call" | custom-call | tf_op jit(solution)/shard_map/cycle/pallas_call | solution.py:606
  43.4 0.7 %copy.5 = f32[3,8,32,128]{3,2,1,0:T(8,128)} copy(f32[3,8,32,128]{3,2,1,0:T(8,128)S(1)} %cycle.1) | data formatting | bytes 786432

commit v6 on v5

--- a/solution.py
+++ b/solution.py
@@ -104,7 +104,7 @@
         remote(sig.at[10:12, 0:32], sig.at[2:4, 0:32], x1, 8, (1, 0)),
         remote(sig.at[4:6, 0:32], sig.at[12:14, 0:32], x1, 9, (-1, 0)),
     ]
-    for copy in second[4:6] + second[0:4] + second[6:8]:
+    for copy in second[0:4] + second[6:8] + second[4:6]:
         copy.start()
     far = (far_send, far_recv)
     later = [
@@ -327,6 +327,8 @@
     for copy in (first[0], first[2], second[0], second[1], second[7]):
         copy.wait()
     unpack(range(8, 11))
+    for copy in later:
+        copy.start()
 
     @pl.when(last_x)
     def _():
@@ -360,8 +362,6 @@
 
     for copy in (first[1], first[3], second[2], second[3], second[6]):
         copy.wait()
-    for copy in later + cs_close:
-        copy.start()
     unpack(range(-4, 0))
 
     @pl.when(first_x)
@@ -380,7 +380,7 @@
     turn_pack[6] = jnp.where(lower, dn[0], jnp.where(sub < 6, roll(dn[1], 4, 0), roll(dn[2], 6, 0)))
     for copy in (swap[4], swap[5], swap[1], swap[6], swap[7]):
         copy.start()
-    for copy in cs_distant:
+    for copy in cs_close + cs_distant:
         copy.start()
 
     for copy in later + swap:

time: 44.2 us -> 42.9 us (0.971)
  Pallas kernels: 43.3 us -> 42 us
    pallas_call x1, Pallas kernels: 43.3 us -> 42 us  [shards(): pl.pallas_call(functools.partial(kernel, nx, ny), out_shape=jax.ShapeDtyp...]
where the time goes in v6:
time: 42.9 us; the launch traced here: 42.8 us
  Pallas kernels  42 us (98%)
  local copies, waits for them, and re-layouts  0.75 us (2%)
    pallas_call x1, Pallas kernels, shards(): pl.pallas_call(functools.partial(kernel, nx, ny), out_shape=jax.ShapeDtyp...  42 us

profile of v6, /device:TPU:1, one launch (start us, length us, event | category | flops | bytes accessed | tf_op | source)
XLA Modules:
  0.0 42.8 jit_solution(8228238684996089871)
XLA Ops:
  0.0 42.0 %cycle.1 = f32[3,8,32,128]{3,2,1,0:T(8,128)S(1)} custom-call(f32[3,8,32,128]{3,2,1,0:T(8,128)} %rhs.1, s32[8,32,128]{2,1,0:T(8,128)} %classes.1, f32[16]{0:T(128)} %table.1), custom_call_target="tpu_custom_call" | custom-call | tf_op jit(solution)/shard_map/cycle/pallas_call | solution.py:606
  42.0 0.7 %copy.5 = f32[3,8,32,128]{3,2,1,0:T(8,128)} copy(f32[3,8,32,128]{3,2,1,0:T(8,128)S(1)} %cycle.1) | data formatting | bytes 786432

commit v7 on v6

--- a/solution.py
+++ b/solution.py
@@ -378,7 +378,7 @@
     turn_pack[5] = jnp.where(lower, roll(up[3], 4, 0), up[2])
     dn = [nod[5 + i, 0:8] for i in range(3)]
     turn_pack[6] = jnp.where(lower, dn[0], jnp.where(sub < 6, roll(dn[1], 4, 0), roll(dn[2], 6, 0)))
-    for copy in (swap[4], swap[5], swap[1], swap[6], swap[7]):
+    for copy in (swap[4], swap[5], swap[6], swap[7], swap[1]):
         copy.start()
     for copy in cs_close + cs_distant:
         copy.start()
@@ -478,7 +478,7 @@
     for x in range(5):
         cf_main[9 + x] = coarse[8 * x:8 * x + 8]
     cf_distant, cf_close = spread(cf_main, cf_pack, cf_got, cf_far, (x3_send, x3_recv), 9, 5)
-    for copy in cf_distant + cf_close:
+    for copy in cf_distant[2:] + cf_close[:4] + cf_distant[:2] + cf_close[6:] + cf_close[4:6]:
         copy.start()
     for copy in cs_distant + cs_close:
         copy.wait()

time: 42.9 us -> 42.2 us (0.984)
  Pallas kernels: 42 us -> 41.2 us
    pallas_call x1, Pallas kernels: 42 us -> 41.2 us  [shards(): pl.pallas_call(functools.partial(kernel, nx, ny), out_shape=jax.ShapeDtyp...]
where the time goes in v7:
time: 42.2 us; the launch traced here: 41.9 us
  Pallas kernels  41.2 us (98%)
  local copies, waits for them, and re-layouts  0.75 us (2%)
    pallas_call x1, Pallas kernels, shards(): pl.pallas_call(functools.partial(kernel, nx, ny), out_shape=jax.ShapeDtyp...  41.2 us

profile of v7, /device:TPU:1, one launch (start us, length us, event | category | flops | bytes accessed | tf_op | source)
XLA Modules:
  0.0 41.9 jit_solution(9786248413825406781)
XLA Ops:
  0.0 41.2 %cycle.1 = f32[3,8,32,128]{3,2,1,0:T(8,128)S(1)} custom-call(f32[3,8,32,128]{3,2,1,0:T(8,128)} %rhs.1, s32[8,32,128]{2,1,0:T(8,128)} %classes.1, f32[16]{0:T(128)} %table.1), custom_call_target="tpu_custom_call" | custom-call | tf_op jit(solution)/shard_map/cycle/pallas_call | solution.py:606
  41.2 0.7 %copy.5 = f32[3,8,32,128]{3,2,1,0:T(8,128)} copy(f32[3,8,32,128]{3,2,1,0:T(8,128)S(1)} %cycle.1) | data formatting | bytes 786432

commit v8 on v7

--- a/solution.py
+++ b/solution.py
@@ -625,7 +625,7 @@
                 pltpu.VMEM((7, 8, 128), f32),
                 pltpu.VMEM((18, ROWS, 128), f32),
                 pltpu.VMEM((9, ROWS, 128), f32),
-                pltpu.VMEM((5, 40, 128), f32),
+                pltpu.VMEM((6, 40, 128), f32),
                 pltpu.VMEM((19, 8, 128), f32),
                 pltpu.VMEM((2, 5, 8, 128), f32),
                 pltpu.VMEM((3, 2, 2, 8, 128), f32),

time: 42.2 us -> 42.2 us (level)
  no operation moved by 1% of the time
where the time goes in v8:
time: 42.2 us; the launch traced here: 41.9 us
  Pallas kernels  41.2 us (98%)
  local copies, waits for them, and re-layouts  0.75 us (2%)
    pallas_call x1, Pallas kernels, shards(): pl.pallas_call(functools.partial(kernel, nx, ny), out_shape=jax.ShapeDtyp...  41.2 us

profile of v8, /device:TPU:1, one launch (start us, length us, event | category | flops | bytes accessed | tf_op | source)
XLA Modules:
  0.0 41.9 jit_solution(13793557058120532223)
XLA Ops:
  0.0 41.2 %cycle.1 = f32[3,8,32,128]{3,2,1,0:T(8,128)S(1)} custom-call(f32[3,8,32,128]{3,2,1,0:T(8,128)} %rhs.1, s32[8,32,128]{2,1,0:T(8,128)} %classes.1, f32[16]{0:T(128)} %table.1), custom_call_target="tpu_custom_call" | custom-call | tf_op jit(solution)/shard_map/cycle/pallas_call | solution.py:606
  41.2 0.7 %copy.5 = f32[3,8,32,128]{3,2,1,0:T(8,128)} copy(f32[3,8,32,128]{3,2,1,0:T(8,128)S(1)} %cycle.1) | data formatting | bytes 786432

commit v9 on v8

--- a/solution.py
+++ b/solution.py
@@ -323,12 +323,12 @@
     edge_turn(0, 1, 6)
     edge_turn(1, 2, 5)
     edge_turn(2, 3, 4)
+    for copy in later:
+        copy.start()
 
     for copy in (first[0], first[2], second[0], second[1], second[7]):
         copy.wait()
     unpack(range(8, 11))
-    for copy in later:
-        copy.start()
 
     @pl.when(last_x)
     def _():

time: 42.2 us -> 42.4 us (level)
  no operation moved by 1% of the time
where the time goes in v9:
time: 42.4 us; the launch traced here: 42.3 us
  Pallas kernels  41.5 us (98%)
  local copies, waits for them, and re-layouts  0.75 us (2%)
    pallas_call x1, Pallas kernels, shards(): pl.pallas_call(functools.partial(kernel, nx, ny), out_shape=jax.ShapeDtyp...  41.5 us

profile of v9, /device:TPU:1, one launch (start us, length us, event | category | flops | bytes accessed | tf_op | source)
XLA Modules:
  0.0 42.3 jit_solution(17730932089461456031)
XLA Ops:
  0.0 41.5 %cycle.1 = f32[3,8,32,128]{3,2,1,0:T(8,128)S(1)} custom-call(f32[3,8,32,128]{3,2,1,0:T(8,128)} %rhs.1, s32[8,32,128]{2,1,0:T(8,128)} %classes.1, f32[16]{0:T(128)} %table.1), custom_call_target="tpu_custom_call" | custom-call | tf_op jit(solution)/shard_map/cycle/pallas_call | solution.py:606
  41.5 0.7 %copy.5 = f32[3,8,32,128]{3,2,1,0:T(8,128)} copy(f32[3,8,32,128]{3,2,1,0:T(8,128)S(1)} %cycle.1) | data formatting | bytes 786432
